TPU v7x, 32 devices: a whole 2x2x4 slice. The times are simulated.
32 devices in a mesh: dp: 8 (over z, y), ctx: 4 (over x, core).
Axes of the slice: x: 2, y: 2, z: 4, core: 2. Of those that a mesh axis runs over, the one named last changes fastest.
Arguments:
- tokens: bfloat16 [16384, 1024], P(('dp', 'ctx'))
- positions: int32 [3, 16384], P(None, ('dp', 'ctx')), may hold values from 0 to 15
- ln1_gain: bfloat16 [1024], P(('dp', 'ctx')), may hold values from 0.25 to 1.75
- ln1_shift: bfloat16 [1024], P(('dp', 'ctx')), may hold values from -4 to 4
- qkv_weight: bfloat16 [1024, 3072], P(('dp', 'ctx')), may hold values from -0.21875 to 0.21875
- qkv_bias: bfloat16 [3072], P(('dp', 'ctx')), may hold values from -4 to 4
- out_weight: bfloat16 [1024, 1024], P(('dp', 'ctx')), may hold values from -0.75 to 0.75
- out_bias: bfloat16 [1024], P(('dp', 'ctx')), may hold values from -4 to 4
- ln2_gain: bfloat16 [1024], P(('dp', 'ctx')), may hold values from 0.25 to 1.75
- ln2_shift: bfloat16 [1024], P(('dp', 'ctx')), may hold values from -4 to 4
- up_weight: bfloat16 [1024, 4096], P(('dp', 'ctx')), may hold values from -0.1875 to 0.1875
- up_bias: bfloat16 [4096], P(('dp', 'ctx')), may hold values from -6 to 6
- down_weight: bfloat16 [4096, 1024], P(('dp', 'ctx')), may hold values from -0.125 to 0.125
- down_bias: bfloat16 [1024], P(('dp', 'ctx')), may hold values from -4 to 4
- cotangent: bfloat16 [16384, 1024], P(('dp', 'ctx')), may hold values from -6 to 6
Outputs:
- output: bfloat16 [16384, 1024], P(('dp', 'ctx'))
- input_grad: float32 [16384, 1024], P(('dp', 'ctx'))
- ln1_gain_grad: float32 [1024], P(('dp', 'ctx'))
- ln1_shift_grad: float32 [1024], P(('dp', 'ctx'))
- qkv_weight_grad: float32 [1024, 3072], P(('dp', 'ctx'))
- qkv_bias_grad: float32 [3072], P(('dp', 'ctx'))
- out_weight_grad: float32 [1024, 1024], P(('dp', 'ctx'))
- out_bias_grad: float32 [1024], P(('dp', 'ctx'))
- ln2_gain_grad: float32 [1024], P(('dp', 'ctx'))
- ln2_shift_grad: float32 [1024], P(('dp', 'ctx'))
- up_weight_grad: float32 [1024, 4096], P(('dp', 'ctx'))
- up_bias_grad: float32 [4096], P(('dp', 'ctx'))
- down_weight_grad: float32 [4096, 1024], P(('dp', 'ctx'))
- down_bias_grad: float32 [1024], P(('dp', 'ctx'))
- norm_stats: float32 [5], replicated
All inputs are finite; a program needn't handle non-finite values.
Results may differ from a plain program's by a relative error of at most 0.014.
Values may be sent and summed in bfloat16 or wider, within the bound.
No kernel may reach another device: no remote copies, remote signals or barrier semaphores. Data moves between devices by JAX's collectives and lax.ppermute only.
A program may use at most 256 MiB of HBM per device.

v0:
```python
import math

import jax
import jax.numpy as jnp
from jax import lax
from jax.sharding import PartitionSpec as P

D = 1024
HD = 64


EPSILON = 1e-06


def layer_norm(values, norm_gain, norm_shift):
    average = jnp.mean(values, axis=-1, keepdims=True)
    centred = values - average
    spread = jnp.mean(centred * centred, axis=-1, keepdims=True)
    return centred * lax.rsqrt(spread + EPSILON) * norm_gain + norm_shift


def gelu_erf(values):
    return 0.5 * values * (1.0 + lax.erf(values * 0.7071067811865476))


def rotary_tables(positions, row_width, head_size):
    pair_gap = head_size // 6
    column = jnp.arange(row_width) % head_size
    segment = column // (2 * pair_gap)
    within = column % (2 * pair_gap)
    freq_index = (within % pair_gap).astype(jnp.float32)
    frequency = jnp.power(10000.0, -freq_index / pair_gap)
    places = positions.astype(jnp.float32)
    angles = jnp.zeros((positions.shape[1], row_width), jnp.float32)
    for axis_num in range(3):
        angles = (
            angles
            + places[axis_num][:, None] * jnp.where(segment == axis_num, frequency, 0.0)[None, :]
        )
    rotated = segment < 3
    cosine_table = jnp.where(rotated, jnp.cos(angles), 1.0)
    sine_table = jnp.where(rotated, jnp.sin(angles), 0.0)
    leading = within < pair_gap
    return (cosine_table, sine_table, leading)


def rotate(values, cosine_table, sine_table, leading, pair_gap):
    partner = jnp.where(
        leading, -jnp.roll(values, -pair_gap, axis=1), jnp.roll(values, pair_gap, axis=1)
    )
    return values * cosine_table + partner * sine_table


def split_groups(matrix):
    return matrix.reshape(matrix.shape[0], -1, 2 * HD).transpose(1, 0, 2)


def join_groups(stacked):
    return stacked.transpose(1, 0, 2).reshape(stacked.shape[1], -1)


def head_scores(q_block, k_group):
    q_heads = q_block.reshape(q_block.shape[0], 2, HD)
    k_heads = k_group.reshape(k_group.shape[0], 2, HD)
    return jnp.einsum("qhd,khd->hqk", q_heads, k_heads, preferred_element_type=jnp.float32)


def forward_block(q_block, k_group, v_group):
    scores = head_scores(q_block, k_group)
    row_top = jnp.max(scores, axis=-1, keepdims=True)
    exponent = jnp.exp(scores - row_top)
    row_total = jnp.sum(exponent, axis=-1, keepdims=True)
    probs_low = (exponent / row_total).astype(jnp.bfloat16)
    v_heads = v_group.reshape(v_group.shape[0], 2, HD)
    mixed_heads = jnp.einsum("hqk,khd->qhd", probs_low, v_heads, preferred_element_type=jnp.float32)
    return (mixed_heads.reshape(q_block.shape[0], 2 * HD), row_top[..., 0], row_total[..., 0])


def backward_block(q_block, grad_block, row_top, row_total, k_group, v_group):
    scores = head_scores(q_block, k_group)
    probs = jnp.exp(scores - row_top[..., None]) / row_total[..., None]
    probs_low = probs.astype(jnp.bfloat16)
    q_heads = q_block.reshape(q_block.shape[0], 2, HD)
    k_heads = k_group.reshape(k_group.shape[0], 2, HD)
    v_heads = v_group.reshape(v_group.shape[0], 2, HD)
    grad_heads = grad_block.reshape(grad_block.shape[0], 2, HD)
    grad_probs = jnp.einsum("qhd,khd->hqk", grad_heads, v_heads, preferred_element_type=jnp.float32)
    inner = jnp.sum(probs * grad_probs, axis=-1, keepdims=True)
    grad_scores = (probs * (grad_probs - inner)).astype(jnp.bfloat16)
    grad_q = jnp.einsum("hqk,khd->qhd", grad_scores, k_heads, preferred_element_type=jnp.float32)
    grad_k = jnp.einsum("hqk,qhd->khd", grad_scores, q_heads, preferred_element_type=jnp.float32)
    grad_v = jnp.einsum("hqk,qhd->khd", probs_low, grad_heads, preferred_element_type=jnp.float32)
    return (
        grad_q.reshape(q_block.shape[0], 2 * HD),
        grad_k.reshape(k_group.shape[0], 2 * HD),
        grad_v.reshape(k_group.shape[0], 2 * HD),
    )


def attend(queries, keys_all, values_all):
    row_count = queries.shape[0]
    block_rows = min(row_count, 512)
    block_count = row_count // block_rows
    group_count = queries.shape[1] // (2 * HD)
    q_groups = split_groups(queries).reshape(group_count, block_count, block_rows, 2 * HD)

    def per_group(operands):
        q_group, k_group, v_group = operands

        def per_block(q_block):
            return forward_block(q_block, k_group, v_group)

        return lax.map(per_block, q_group)

    mixed_heads, row_tops, row_totals = lax.map(
        per_group, (q_groups, split_groups(keys_all), split_groups(values_all))
    )
    return (join_groups(mixed_heads.reshape(group_count, row_count, 2 * HD)), row_tops, row_totals)


def attend_back(queries, grad_mixed, row_tops, row_totals, keys_all, values_all):
    row_count = queries.shape[0]
    block_rows = min(row_count, 512)
    block_count = row_count // block_rows
    group_count = queries.shape[1] // (2 * HD)
    q_groups = split_groups(queries).reshape(group_count, block_count, block_rows, 2 * HD)
    g_groups = split_groups(grad_mixed).reshape(group_count, block_count, block_rows, 2 * HD)

    def per_group(operands):
        q_group, g_group, top_group, total_group, k_group, v_group = operands

        def per_block(carried, block_ops):
            k_acc, v_acc = carried
            q_block, g_block, row_top, row_total = block_ops
            grad_q, grad_k, grad_v = backward_block(
                q_block, g_block, row_top, row_total, k_group, v_group
            )
            return ((k_acc + grad_k, v_acc + grad_v), grad_q)

        zeros_init = jnp.zeros(k_group.shape, jnp.float32)
        (grad_k, grad_v), grad_q = lax.scan(
            per_block, (zeros_init, zeros_init), (q_group, g_group, top_group, total_group)
        )
        return (grad_q, grad_k, grad_v)

    grad_q, grad_k, grad_v = lax.map(
        per_group,
        (
            q_groups,
            g_groups,
            row_tops,
            row_totals,
            split_groups(keys_all),
            split_groups(values_all),
        ),
    )
    return (
        join_groups(grad_q.reshape(group_count, row_count, 2 * HD)),
        join_groups(grad_k),
        join_groups(grad_v),
    )


def per_device(
    tokens,
    positions,
    ln1_gain,
    ln1_shift,
    qkv_weight,
    qkv_bias,
    out_weight,
    out_bias,
    ln2_gain,
    ln2_shift,
    up_weight,
    up_bias,
    down_weight,
    down_bias,
    cotangent,
):
    pair_gap = HD // 6
    scaling = 1.0 / math.sqrt(HD)
    attn_params = (
        lax.all_gather(ln1_gain, ("dp", "ctx"), axis=0, tiled=True),
        lax.all_gather(ln1_shift, ("dp", "ctx"), axis=0, tiled=True),
        lax.all_gather(qkv_weight, ("dp", "ctx"), axis=0, tiled=True),
        lax.all_gather(qkv_bias, ("dp", "ctx"), axis=0, tiled=True),
        lax.all_gather(out_weight, ("dp", "ctx"), axis=0, tiled=True),
        lax.all_gather(out_bias, ("dp", "ctx"), axis=0, tiled=True),
    )
    mlp_params = (
        lax.all_gather(ln2_gain, ("dp", "ctx"), axis=0, tiled=True),
        lax.all_gather(ln2_shift, ("dp", "ctx"), axis=0, tiled=True),
        lax.all_gather(up_weight, ("dp", "ctx"), axis=0, tiled=True),
        lax.all_gather(up_bias, ("dp", "ctx"), axis=0, tiled=True),
        lax.all_gather(down_weight, ("dp", "ctx"), axis=0, tiled=True),
        lax.all_gather(down_bias, ("dp", "ctx"), axis=0, tiled=True),
    )
    gain_one = attn_params[0].astype(jnp.float32)
    shift_one = attn_params[1].astype(jnp.float32)
    gain_two = mlp_params[0].astype(jnp.float32)
    shift_two = mlp_params[1].astype(jnp.float32)
    inputs_f = tokens.astype(jnp.float32)
    normed = layer_norm(inputs_f, gain_one, shift_one)
    normed_low = normed.astype(jnp.bfloat16)
    joined = jnp.dot(normed_low, attn_params[2], preferred_element_type=jnp.float32) + attn_params[
        3
    ].astype(jnp.float32)
    cosine_table, sine_table, leading = rotary_tables(positions, D, HD)

    def turn_query(part):
        return rotate(part, cosine_table, sine_table, leading, pair_gap) * scaling

    def turn_key(part):
        return rotate(part, cosine_table, sine_table, leading, pair_gap)

    query_part = joined[:, :D]
    key_part = joined[:, D : 2 * D]
    queries = turn_query(query_part).astype(jnp.bfloat16)
    keys_low = turn_key(key_part).astype(jnp.bfloat16)
    values_low = joined[:, 2 * D :].astype(jnp.bfloat16)
    keys_all, values_all = (
        lax.all_gather(keys_low, "ctx", axis=0, tiled=True),
        lax.all_gather(values_low, "ctx", axis=0, tiled=True),
    )
    mixed_heads, row_tops, row_totals = attend(queries, keys_all, values_all)
    mixed_low = mixed_heads.astype(jnp.bfloat16)
    attn_out = jnp.dot(mixed_low, attn_params[4], preferred_element_type=jnp.float32) + attn_params[
        5
    ].astype(jnp.float32)
    middle = inputs_f + attn_out
    normed_two = layer_norm(middle, gain_two, shift_two)
    normed_two_low = normed_two.astype(jnp.bfloat16)
    upward = jnp.dot(
        normed_two_low, mlp_params[2], preferred_element_type=jnp.float32
    ) + mlp_params[3].astype(jnp.float32)
    active_low = gelu_erf(upward).astype(jnp.bfloat16)
    mlp_out = jnp.dot(active_low, mlp_params[4], preferred_element_type=jnp.float32) + mlp_params[
        5
    ].astype(jnp.float32)
    final_out = middle + mlp_out
    squares = jnp.stack(
        [
            jnp.sum(inputs_f * inputs_f),
            jnp.sum(attn_out * attn_out),
            jnp.sum(middle * middle),
            jnp.sum(mlp_out * mlp_out),
            jnp.sum(final_out * final_out),
        ]
    )
    square_totals = lax.psum(squares, ("dp", "ctx"))
    entry_count = tokens.shape[0] * lax.axis_size(("dp", "ctx")) * D
    norm_stats = jnp.sqrt(square_totals / entry_count)
    mlp_back = (
        lax.all_gather(ln2_gain, ("dp", "ctx"), axis=0, tiled=True),
        lax.all_gather(ln2_shift, ("dp", "ctx"), axis=0, tiled=True),
        lax.all_gather(up_weight, ("dp", "ctx"), axis=0, tiled=True),
        lax.all_gather(up_bias, ("dp", "ctx"), axis=0, tiled=True),
        lax.all_gather(down_weight, ("dp", "ctx"), axis=0, tiled=True),
        lax.all_gather(down_bias, ("dp", "ctx"), axis=0, tiled=True),
    )
    grad_final = cotangent.astype(jnp.float32)
    grad_mlp = grad_final.astype(jnp.bfloat16)
    down_grad = jnp.einsum("tf,td->fd", active_low, grad_mlp, preferred_element_type=jnp.float32)
    down_bias_grad = jnp.sum(grad_mlp.astype(jnp.float32), axis=0)
    grad_active = jnp.einsum("td,fd->tf", grad_mlp, mlp_back[4], preferred_element_type=jnp.float32)
    gelu_pull = jax.vjp(gelu_erf, upward)[1]
    grad_up = gelu_pull(grad_active)[0].astype(jnp.bfloat16)
    up_grad = jnp.einsum("tm,tf->mf", normed_two_low, grad_up, preferred_element_type=jnp.float32)
    up_bias_grad = jnp.sum(grad_up.astype(jnp.float32), axis=0)
    grad_normed_two = jnp.einsum(
        "tf,mf->tm", grad_up, mlp_back[2], preferred_element_type=jnp.float32
    )
    norm_pull_two = jax.vjp(
        layer_norm, middle, mlp_back[0].astype(jnp.float32), mlp_back[1].astype(jnp.float32)
    )[1]
    grad_middle_norm, gain_two_grad, shift_two_grad = norm_pull_two(grad_normed_two)
    grad_middle = grad_final + grad_middle_norm
    mlp_terms = (gain_two_grad, shift_two_grad, up_grad, up_bias_grad, down_grad, down_bias_grad)
    mlp_grads = (
        lax.psum_scatter(mlp_terms[0], ("dp", "ctx"), scatter_dimension=0, tiled=True),
        lax.psum_scatter(mlp_terms[1], ("dp", "ctx"), scatter_dimension=0, tiled=True),
        lax.psum_scatter(mlp_terms[2], ("dp", "ctx"), scatter_dimension=0, tiled=True),
        lax.psum_scatter(mlp_terms[3], ("dp", "ctx"), scatter_dimension=0, tiled=True),
        lax.psum_scatter(mlp_terms[4], ("dp", "ctx"), scatter_dimension=0, tiled=True),
        lax.psum_scatter(mlp_terms[5], ("dp", "ctx"), scatter_dimension=0, tiled=True),
    )
    attn_back = (
        lax.all_gather(ln1_gain, ("dp", "ctx"), axis=0, tiled=True),
        lax.all_gather(ln1_shift, ("dp", "ctx"), axis=0, tiled=True),
        lax.all_gather(qkv_weight, ("dp", "ctx"), axis=0, tiled=True),
        lax.all_gather(qkv_bias, ("dp", "ctx"), axis=0, tiled=True),
        lax.all_gather(out_weight, ("dp", "ctx"), axis=0, tiled=True),
        lax.all_gather(out_bias, ("dp", "ctx"), axis=0, tiled=True),
    )
    grad_attn = grad_middle.astype(jnp.bfloat16)
    out_grad = jnp.einsum("tm,td->md", mixed_low, grad_attn, preferred_element_type=jnp.float32)
    out_bias_grad = jnp.sum(grad_attn.astype(jnp.float32), axis=0)
    grad_mixed = jnp.einsum(
        "td,md->tm", grad_attn, attn_back[4], preferred_element_type=jnp.float32
    ).astype(jnp.bfloat16)
    grad_q, grad_k_all, grad_v_all = attend_back(
        queries, grad_mixed, row_tops, row_totals, keys_all, values_all
    )
    grad_k, grad_v = (
        lax.psum_scatter(
            grad_k_all.astype(jnp.bfloat16), "ctx", scatter_dimension=0, tiled=True
        ).astype(jnp.float32),
        lax.psum_scatter(
            grad_v_all.astype(jnp.bfloat16), "ctx", scatter_dimension=0, tiled=True
        ).astype(jnp.float32),
    )
    query_pull = jax.vjp(turn_query, query_part)[1]
    key_pull = jax.vjp(turn_key, key_part)[1]
    grad_joined = jnp.concatenate(
        [query_pull(grad_q)[0], key_pull(grad_k)[0], grad_v], axis=1
    ).astype(jnp.bfloat16)
    qkv_grad = jnp.einsum("tm,tc->mc", normed_low, grad_joined, preferred_element_type=jnp.float32)
    qkv_bias_grad = jnp.sum(grad_joined.astype(jnp.float32), axis=0)
    grad_normed = jnp.einsum(
        "tc,mc->tm", grad_joined, attn_back[2], preferred_element_type=jnp.float32
    )
    norm_pull_one = jax.vjp(
        layer_norm, inputs_f, attn_back[0].astype(jnp.float32), attn_back[1].astype(jnp.float32)
    )[1]
    grad_inputs_norm, gain_one_grad, shift_one_grad = norm_pull_one(grad_normed)
    input_grad = grad_middle + grad_inputs_norm
    attn_terms = (gain_one_grad, shift_one_grad, qkv_grad, qkv_bias_grad, out_grad, out_bias_grad)
    attn_grads = (
        lax.psum_scatter(attn_terms[0], ("dp", "ctx"), scatter_dimension=0, tiled=True),
        lax.psum_scatter(attn_terms[1], ("dp", "ctx"), scatter_dimension=0, tiled=True),
        lax.psum_scatter(attn_terms[2], ("dp", "ctx"), scatter_dimension=0, tiled=True),
        lax.psum_scatter(attn_terms[3], ("dp", "ctx"), scatter_dimension=0, tiled=True),
        lax.psum_scatter(attn_terms[4], ("dp", "ctx"), scatter_dimension=0, tiled=True),
        lax.psum_scatter(attn_terms[5], ("dp", "ctx"), scatter_dimension=0, tiled=True),
    )
    return (
        final_out.astype(jnp.bfloat16),
        input_grad,
        attn_grads[0],
        attn_grads[1],
        attn_grads[2],
        attn_grads[3],
        attn_grads[4],
        attn_grads[5],
        mlp_grads[0],
        mlp_grads[1],
        mlp_grads[2],
        mlp_grads[3],
        mlp_grads[4],
        mlp_grads[5],
        norm_stats,
    )


def solution(mesh):
    in_specs = (
        P(("dp", "ctx"), None),
        P(None, ("dp", "ctx")),
        P(("dp", "ctx")),
        P(("dp", "ctx")),
        P(("dp", "ctx"), None),
        P(("dp", "ctx")),
        P(("dp", "ctx"), None),
        P(("dp", "ctx")),
        P(("dp", "ctx")),
        P(("dp", "ctx")),
        P(("dp", "ctx"), None),
        P(("dp", "ctx")),
        P(("dp", "ctx"), None),
        P(("dp", "ctx")),
        P(("dp", "ctx"), None),
    )
    out_specs = (
        P(("dp", "ctx"), None),
        P(("dp", "ctx"), None),
        P(("dp", "ctx")),
        P(("dp", "ctx")),
        P(("dp", "ctx"), None),
        P(("dp", "ctx")),
        P(("dp", "ctx"), None),
        P(("dp", "ctx")),
        P(("dp", "ctx")),
        P(("dp", "ctx")),
        P(("dp", "ctx"), None),
        P(("dp", "ctx")),
        P(("dp", "ctx"), None),
        P(("dp", "ctx")),
        P(),
    )
    return jax.shard_map(
        per_device, mesh=mesh, in_specs=in_specs, out_specs=out_specs, check_vma=False
    )
```

profile of v0, /device:TPU:0, one launch (start us, length us, event | category | flops | bytes accessed | tf_op | source)
XLA Modules:
  0.0 1375.9 jit_solution(10352610235294406713)
XLA Ops:
  13.9 42.4 %all-reduce.24 = (bf16[3072]{0:T(1024)(128)(2,1)S(1)}, bf16[1024]{0:T(1024)(128)(2,1)S(1)}, bf16[1024]{0:T(1024)(128)(2,1)S(1)}, bf16[1024]{0:T(1024)(128)(2,1)S...) all-reduce(bf16[3072]{0:T(1024)(128)(2,1)S(1)} %dynamic-update-slic, ...), channel_id=1, replica_groups=mesh['dp'=8,'ctx'=4] {'dp','ctx'}, use_global_device_ids=true, to_apply=%add.10 | all-reduce | flops 9216 | bytes 36864
  59.1 24.1 %all-gather.8.cloned.1.call-done = bf16[1024,3072]{1,0:T(8,128)(2,1)} async-done(((bf16[32,3072]{1,0:T(8,128)(2,1)}), bf16[1024,3072]{1,0:T(8,128)(2,1)}) %all-gather.8.cloned.1.call-update) | async-done | bytes 6291472 | tf_op jit(solution)/shard_map/all_gather | solution.py:186
  83.2 5.8 convolution_add_fusion
  91.8 10.6 fusion.20
  108.1 39.0 %all-gather = bf16[32,1,128]{2,1,0:T(2,128)(2,1)S(1)} all-gather(bf16[1,1,128]{2,1,0:T(2,128)(2,1)S(1)} %bitcast.210), channel_id=1, replica_groups=mesh['dp'=8,'ctx'=4] {'dp','ctx'}, dimensions={0}, use_global_device_ids=true | all-gather | bytes 8448 | tf_op jit(solution)/shard_map/all_gather | solution.py:195
  147.7 6.6 copy.46
  154.3 17.4 %all-gather.10.cloned.1.call-done = bf16[2048,1024]{1,0:T(8,128)(2,1)} async-done(((bf16[512,1024]{1,0:T(8,128)(2,1)}), bf16[2048,1024]{1,0:T(8,128)(2,1)}) %all-gather.10.cloned.1.call-update) | async-done | bytes 4194320 | tf_op jit(solution)/shard_map/all_gather | solution.py:224
  171.7 6.5 copy.44
  178.3 56.2 %while.30 = (s32[]{:T(128)}, bf16[8,1,512,128]{2,3,1,0:T(8,128)(2,1)S(1)}, f32[8,1,2,512]{3,2,1,0:T(2,128)S(1)}, f32[8,1,2,512]{3,2,1,0:T(2,128)S(1)}, bf16[8,20...) while((s32[]{:T(128)}, ...), condition=%wide.region_5.6_spmd.clone, body=%wide.region_2.5_spmd.sunk.clone | while | flops 549451776 | bytes 29134944 | solution.py:115
  235.7 4.1 fusion.58
  240.2 69.7 %all-gather.16.cloned.1.call-done = bf16[1024,4096]{1,0:T(8,128)(2,1)} async-done(((bf16[32,4096]{1,0:T(8,128)(2,1)}), bf16[1024,4096]{1,0:T(8,128)(2,1)}) %all-gather.16.cloned.1.call-update) | async-done | bytes 8388624 | tf_op jit(solution)/shard_map/all_gather | solution.py:194
  310.0 10.3 fusion.54
  320.3 68.5 %all-gather.18.cloned.1.call-done = bf16[4096,1024]{1,0:T(8,128)(2,1)} async-done(((bf16[128,1024]{1,0:T(8,128)(2,1)}), bf16[4096,1024]{1,0:T(8,128)(2,1)}) %all-gather.18.cloned.1.call-update) | async-done | bytes 8388624 | tf_op jit(solution)/shard_map/all_gather | solution.py:196
  388.8 14.9 %convert_reduce_fusion = (f32[4096]{0:T(1024)}, bf16[512,4096]{1,0:T(8,128)(2,1)}, bf16[512,4096]{1,0:T(8,128)(2,1)}) fusion(f32[512,4096]{1,0:T(8,128)} %fusion.54, f32[4096]{0:T(1024)S(1)} %bitcast.209, bf16[512,1024]{1,0:T(8,128)(2,1)S(1)} %copy-done.13, bf16[4096,1024]{1,0:T(8,128)(2,1)} %all-gather.18.cloned.1.call-done), kind=kOutput, calls=%fused_computation.24 | convolution fusion | flops 4332711936 | bytes 26247168 | tf_op jit(solution)/shard_map/td,fd->tf/dot_general | solution.py:266
  403.7 7.2 fusion.66
  411.0 9.3 multiply_reduce_fusion.1
  425.4 172.4 %while.31 = (s32[]{:T(128)}, f32[8,1,512,128]{2,3,1,0:T(8,128)}, bf16[8,2048,128]{1,2,0:T(8,128)(2,1)}, bf16[8,2048,128]{1,2,0:T(8,128)(2,1)}, bf16[8,2048,128]{...) while((s32[]{:T(128)}, f32[8,1,512,128]{2,3,1,0:T(8,128)}, ...), condition=%wide.region_12.13_spmd.clone, body=%wide.region_10.12_spmd.sunk.clone | while | flops 1358953472 | bytes 147097312 | solution.py:146
  429.6 5.2 multiply_reduce_fusion.10
  435.3 6.6 multiply_convert_fusion.4
  451.1 5.2 multiply_reduce_fusion.10
  456.8 6.6 multiply_convert_fusion.4
  472.6 5.2 multiply_reduce_fusion.10
  478.3 6.6 multiply_convert_fusion.4
  494.1 5.2 multiply_reduce_fusion.10
  499.8 6.6 multiply_convert_fusion.4
  515.6 5.2 multiply_reduce_fusion.10
  521.3 6.6 multiply_convert_fusion.4
  537.1 5.2 multiply_reduce_fusion.10
  542.8 6.6 multiply_convert_fusion.4
  558.6 5.2 multiply_reduce_fusion.10
  564.3 6.6 multiply_convert_fusion.4
  580.0 5.2 multiply_reduce_fusion.10
  585.7 6.6 multiply_convert_fusion.4
  597.8 6.4 copy.49
  604.3 6.5 copy.50
  621.6 25.9 %reduce-scatter.7.cloned.1.call-done = bf16[512,1024]{1,0:T(8,128)(2,1)} async-done(((bf16[2048,1024]{1,0:T(8,128)(2,1)}), bf16[512,1024]{1,0:T(8,128)(2,1)}) %reduce-scatter.7.cloned.1.call-update) | async-done | bytes 1048592 | tf_op jit(solution)/shard_map/reduce_scatter | solution.py:306
  647.6 9.3 fusion.31
  659.1 9.6 add_convert_fusion.1
  668.7 26.1 %reduce-scatter.9.cloned.1.call-done = bf16[512,1024]{1,0:T(8,128)(2,1)} async-done(((bf16[2048,1024]{1,0:T(8,128)(2,1)}), bf16[512,1024]{1,0:T(8,128)(2,1)}) %reduce-scatter.9.cloned.1.call-update) | async-done | bytes 1048592 | tf_op jit(solution)/shard_map/reduce_scatter | solution.py:309
  694.8 10.0 fusion.48
  706.4 10.5 fusion.53
  718.1 10.7 fusion.68
  730.3 8.7 fusion.55
  749.1 40.8 %all-reduce.23 = (f32[1024]{0:T(1024)S(1)}, f32[1024]{0:T(1024)S(1)}, f32[3072]{0:T(1024)S(1)}, f32[1024]{0:T(1024)S(1)}, f32[1024]{0:T(1024)S(1)}, /*index=5*/f...) all-reduce(f32[1024]{0:T(1024)S(1)} %get-tuple-element.167, ...), channel_id=4, replica_groups=mesh['dp'=8,'ctx'=4] {'dp','ctx'}, use_global_device_ids=true, to_apply=%region_18.19.clone | all-reduce | flops 13317 | bytes 106536
  795.1 43.6 %reduce-scatter.13.cloned.1.call-done = f32[32,1024]{1,0:T(8,128)} async-done(((f32[1024,1024]{1,0:T(8,128)}), f32[32,1024]{1,0:T(8,128)}) %reduce-scatter.13.cloned.1.call-update) | async-done | bytes 131088 | tf_op jit(solution)/shard_map/reduce_scatter | solution.py:334
  838.7 157.9 %reduce-scatter.11.cloned.1.call-done = f32[32,3072]{1,0:T(8,128)} async-done(((f32[1024,3072]{1,0:T(8,128)}), f32[32,3072]{1,0:T(8,128)}) %reduce-scatter.11.cloned.1.call-update) | async-done | bytes 393232 | tf_op jit(solution)/shard_map/reduce_scatter | solution.py:332
  996.6 184.8 %reduce-scatter.15.cloned.1.call-done = f32[32,4096]{1,0:T(8,128)} async-done(((f32[1024,4096]{1,0:T(8,128)}), f32[32,4096]{1,0:T(8,128)}) %reduce-scatter.15.cloned.1.call-update) | async-done | bytes 524304 | tf_op jit(solution)/shard_map/reduce_scatter | solution.py:283
  1181.4 187.4 %reduce-scatter.17.cloned.1.call-done = f32[128,1024]{1,0:T(8,128)} async-done(((f32[4096,1024]{1,0:T(8,128)}), f32[128,1024]{1,0:T(8,128)}) %reduce-scatter.17.cloned.1.call-update) | async-done | bytes 524304 | tf_op jit(solution)/shard_map/reduce_scatter | solution.py:285
  (438 shorter events, 190.4 us)
Async XLA Ops:
  7.2 51.4 %copy-start.2 = (bf16[512,1024]{1,0:T(8,128)(2,1)S(1)}, bf16[512,1024]{1,0:T(8,128)(2,1)}, u32[]{:S(2)}) copy-start(bf16[512,1024]{1,0:T(8,128)(2,1)} %param.19) | copy-start | bytes 3145732
  7.2 76.0 %all-gather.8.cloned.1.call-start = ((), (), s32[]{:S(2)}) async-start(), calls=%async_computation.6 | async-start | bytes 6488064 | tf_op jit(solution)/shard_map/all_gather | solution.py:186
  7.9 139.8 %all-gather.12.cloned.1.call-start = ((), (), s32[]{:S(2)}) async-start(), calls=%async_computation.8 | async-start | bytes 5242880 | tf_op jit(solution)/shard_map/all_gather | solution.py:223
  56.3 32.7 %copy-start.26 = (f32[1024]{0:T(1024)}, f32[1024]{0:T(1024)S(1)}, u32[]{:S(2)}) copy-start(f32[1024]{0:T(1024)S(1)} %convert_element_type.139) | copy-start | bytes 12292
  56.3 32.7 %copy-start.28 = (f32[1024]{0:T(1024)}, f32[1024]{0:T(1024)S(1)}, u32[]{:S(2)}) copy-start(f32[1024]{0:T(1024)S(1)} %convert_element_type.140) | copy-start | bytes 12292
  57.1 33.9 %copy-start.56 = (pred[1024]{0:T(1024)(128)(4,1)}, pred[1024]{0:T(1024)(128)(4,1)S(1)}, u32[]{:S(2)}) copy-start(pred[1024]{0:T(1024)(128)(4,1)S(1)} %get-tuple-element.278) | copy-start | bytes 3076
  57.1 33.9 %copy-start.58 = (pred[1024]{0:T(1024)(128)(4,1)}, pred[1024]{0:T(1024)(128)(4,1)S(1)}, u32[]{:S(2)}) copy-start(pred[1024]{0:T(1024)(128)(4,1)S(1)} %get-tuple-element.277) | copy-start | bytes 3076
  57.1 33.8 %copy-start.34 = (f32[1024]{0:T(1024)}, f32[1024]{0:T(1024)S(1)}, u32[]{:S(2)}) copy-start(f32[1024]{0:T(1024)S(1)} %compare_select_fusion.2) | copy-start | bytes 12292
  57.1 33.8 %copy-start.36 = (f32[1024]{0:T(1024)}, f32[1024]{0:T(1024)S(1)}, u32[]{:S(2)}) copy-start(f32[1024]{0:T(1024)S(1)} %get-tuple-element.275) | copy-start | bytes 12292
  57.1 33.8 %copy-start.38 = (f32[1024]{0:T(1024)}, f32[1024]{0:T(1024)S(1)}, u32[]{:S(2)}) copy-start(f32[1024]{0:T(1024)S(1)} %get-tuple-element.276) | copy-start | bytes 12292
  58.6 30.4 %copy-start.30 = (f32[512]{0:T(512)}, f32[512]{0:T(512)S(1)}, u32[]{:S(2)}) copy-start(f32[512]{0:T(512)S(1)} %broadcast_multiply_fusion.2) | copy-start | bytes 6148
  59.0 30.0 %copy-start.48 = (f32[512]{0:T(512)}, f32[512]{0:T(512)S(1)}, u32[]{:S(2)}) copy-start(f32[512]{0:T(512)S(1)} %fusion.16) | copy-start | bytes 6148
  59.1 30.0 %copy-start.32 = (f32[512]{0:T(512)}, f32[512]{0:T(512)S(1)}, u32[]{:S(2)}) copy-start(f32[512]{0:T(512)S(1)} %fusion.46) | copy-start | bytes 6148
  59.1 31.9 %copy-start.40 = (f32[1,512]{1,0:T(1,128)}, f32[1,512]{1,0:T(1,128)S(1)}, u32[]{:S(2)}) copy-start(f32[1,512]{1,0:T(1,128)S(1)} %get-tuple-element.271) | copy-start | bytes 6148
  59.1 31.9 %copy-start.42 = (f32[1,512]{1,0:T(1,128)}, f32[1,512]{1,0:T(1,128)S(1)}, u32[]{:S(2)}) copy-start(f32[1,512]{1,0:T(1,128)S(1)} %get-tuple-element.272) | copy-start | bytes 6148
  59.1 31.9 %copy-start.44 = (f32[1,512]{1,0:T(1,128)}, f32[1,512]{1,0:T(1,128)S(1)}, u32[]{:S(2)}) copy-start(f32[1,512]{1,0:T(1,128)S(1)} %get-tuple-element.273) | copy-start | bytes 6148
  102.4 69.4 %all-gather.10.cloned.1.call-start = ((), (), s32[]{:S(2)}) async-start(), calls=%async_computation.7 | async-start | bytes 5242880 | tf_op jit(solution)/shard_map/all_gather | solution.py:224
  105.2 129.3 %all-gather.14.cloned.1.call-start = ((), (), s32[]{:S(2)}) async-start(), calls=%async_computation.9 | async-start | bytes 2162688 | tf_op jit(solution)/shard_map/all_gather | solution.py:188
  105.7 204.2 %all-gather.16.cloned.1.call-start = ((), (), s32[]{:S(2)}) async-start(), calls=%async_computation.10 | async-start | bytes 8650752 | tf_op jit(solution)/shard_map/all_gather | solution.py:194
  106.3 282.4 %all-gather.18.cloned.1.call-start = ((), (), s32[]{:S(2)}) async-start(), calls=%async_computation.11 | async-start | bytes 8650752 | tf_op jit(solution)/shard_map/all_gather | solution.py:196
  106.9 540.6 %reduce-scatter.7.cloned.1.call-start = ((), (), s32[]{:S(2)}) async-start(), calls=%async_computation.12 | async-start | bytes 5242880 | tf_op jit(solution)/shard_map/reduce_scatter | solution.py:306
  108.0 312.3 %copy-start.54 = (f32[1024]{0:T(1024)}, f32[1024]{0:T(1024)S(1)}, u32[]{:S(2)}) copy-start(f32[1024]{0:T(1024)S(1)} %convert_element_type.152) | copy-start | bytes 12292
  108.0 201.9 %copy-start.62 = (f32[1024]{0:T(1024)}, f32[1024]{0:T(1024)S(1)}, u32[]{:S(2)}) copy-start(f32[1024]{0:T(1024)S(1)} %convert_element_type.153) | copy-start | bytes 12292
  154.3 24.0 %copy-start.17 = (bf16[8,1,512,128]{2,3,1,0:T(8,128)(2,1)S(1)}, bf16[8,1,512,128]{2,3,1,0:T(8,128)(2,1)}, u32[]{:S(2)}) copy-start(bf16[8,1,512,128]{2,3,1,0:T(8,128)(2,1)} %broadcast_convert_fusion) | copy-start | bytes 3145732
  239.9 180.5 %copy-start.7 = (f32[512,1024]{1,0:T(8,128)}, f32[512,1024]{1,0:T(8,128)S(1)}, u32[]{:S(2)}) copy-start(f32[512,1024]{1,0:T(8,128)S(1)} %get-tuple-element.235) | copy-start | bytes 6291460
  239.9 180.5 %copy-start.50 = (f32[512]{0:T(512)}, f32[512]{0:T(512)S(1)}, u32[]{:S(2)}) copy-start(f32[512]{0:T(512)S(1)} %broadcast_multiply_fusion.1) | copy-start | bytes 6148
  240.2 180.1 %copy-start.60 = (f32[512]{0:T(512)}, f32[512]{0:T(512)S(1)}, u32[]{:S(2)}) copy-start(f32[512]{0:T(512)S(1)} %fusion.47) | copy-start | bytes 6148
  240.2 148.5 %copy-start.13 = (bf16[512,1024]{1,0:T(8,128)(2,1)S(1)}, bf16[512,1024]{1,0:T(8,128)(2,1)}, u32[]{:S(2)}) copy-start(bf16[512,1024]{1,0:T(8,128)(2,1)} %param.33) | copy-start | bytes 3145732
  388.8 15.0 %copy-start.68 = (bf16[1024,4096]{1,0:T(8,128)(2,1)S(1)}, bf16[1024,4096]{1,0:T(8,128)(2,1)}, u32[]{:S(2)}) copy-start(bf16[1024,4096]{1,0:T(8,128)(2,1)} %all-gather.16.cloned.1.call-done) | copy-start | bytes 25165828
  604.3 90.5 %reduce-scatter.9.cloned.1.call-start = ((), (), s32[]{:S(2)}) async-start(), calls=%async_computation.13 | async-start | bytes 5242880 | tf_op jit(solution)/shard_map/reduce_scatter | solution.py:309
  610.8 227.9 %reduce-scatter.13.cloned.1.call-start = ((), (), s32[]{:S(2)}) async-start(), calls=%async_computation.15 | async-start | bytes 4325376 | tf_op jit(solution)/shard_map/reduce_scatter | solution.py:334
  616.2 380.4 %reduce-scatter.11.cloned.1.call-start = ((), (), s32[]{:S(2)}) async-start(), calls=%async_computation.14 | async-start | bytes 12976128 | tf_op jit(solution)/shard_map/reduce_scatter | solution.py:332
  619.5 28.1 %copy-start.35 = (f32[1024]{0:T(1024)S(1)}, f32[1024]{0:T(1024)}, u32[]{:S(2)}) copy-start(f32[1024]{0:T(1024)} %copy-done.34) | copy-start | bytes 12292
  619.5 28.1 %copy-start.37 = (f32[1024]{0:T(1024)S(1)}, f32[1024]{0:T(1024)}, u32[]{:S(2)}) copy-start(f32[1024]{0:T(1024)} %copy-done.36) | copy-start | bytes 12292
  619.5 28.1 %copy-start.39 = (f32[1024]{0:T(1024)S(1)}, f32[1024]{0:T(1024)}, u32[]{:S(2)}) copy-start(f32[1024]{0:T(1024)} %copy-done.38) | copy-start | bytes 12292
  619.5 28.1 %copy-start.41 = (f32[1,512]{1,0:T(1,128)S(1)}, f32[1,512]{1,0:T(1,128)}, u32[]{:S(2)}) copy-start(f32[1,512]{1,0:T(1,128)} %copy-done.40) | copy-start | bytes 6148
  619.5 28.1 %copy-start.43 = (f32[1,512]{1,0:T(1,128)S(1)}, f32[1,512]{1,0:T(1,128)}, u32[]{:S(2)}) copy-start(f32[1,512]{1,0:T(1,128)} %copy-done.42) | copy-start | bytes 6148
  619.5 28.1 %copy-start.45 = (f32[1,512]{1,0:T(1,128)S(1)}, f32[1,512]{1,0:T(1,128)}, u32[]{:S(2)}) copy-start(f32[1,512]{1,0:T(1,128)} %copy-done.44) | copy-start | bytes 6148
  619.5 28.1 %copy-start.57 = (pred[1024]{0:T(1024)(128)(4,1)S(1)}, pred[1024]{0:T(1024)(128)(4,1)}, u32[]{:S(2)}) copy-start(pred[1024]{0:T(1024)(128)(4,1)} %copy-done.56) | copy-start | bytes 3076
  619.5 28.1 %copy-start.59 = (pred[1024]{0:T(1024)(128)(4,1)S(1)}, pred[1024]{0:T(1024)(128)(4,1)}, u32[]{:S(2)}) copy-start(pred[1024]{0:T(1024)(128)(4,1)} %copy-done.58) | copy-start | bytes 3076
  659.0 35.7 %copy-start.3 = (bf16[512,1024]{1,0:T(8,128)(2,1)S(1)}, bf16[512,1024]{1,0:T(8,128)(2,1)}, u32[]{:S(2)}) copy-start(bf16[512,1024]{1,0:T(8,128)(2,1)} %param.19) | copy-start | bytes 3145732
  659.0 35.7 %copy-start.27 = (f32[1024]{0:T(1024)S(1)}, f32[1024]{0:T(1024)}, u32[]{:S(2)}) copy-start(f32[1024]{0:T(1024)} %copy-done.26) | copy-start | bytes 12292
  659.0 35.7 %copy-start.29 = (f32[1024]{0:T(1024)S(1)}, f32[1024]{0:T(1024)}, u32[]{:S(2)}) copy-start(f32[1024]{0:T(1024)} %copy-done.28) | copy-start | bytes 12292
  659.0 35.7 %copy-start.31 = (f32[512]{0:T(512)S(1)}, f32[512]{0:T(512)}, u32[]{:S(2)}) copy-start(f32[512]{0:T(512)} %copy-done.30) | copy-start | bytes 6148
  659.0 35.7 %copy-start.33 = (f32[512]{0:T(512)S(1)}, f32[512]{0:T(512)}, u32[]{:S(2)}) copy-start(f32[512]{0:T(512)} %copy-done.32) | copy-start | bytes 6148
  704.8 476.6 %reduce-scatter.15.cloned.1.call-start = ((), (), s32[]{:S(2)}) async-start(), calls=%async_computation.16 | async-start | bytes 17301504 | tf_op jit(solution)/shard_map/reduce_scatter | solution.py:283
  716.9 651.9 %reduce-scatter.17.cloned.1.call-start = ((), (), s32[]{:S(2)}) async-start(), calls=%async_computation.17 | async-start | bytes 17301504 | tf_op jit(solution)/shard_map/reduce_scatter | solution.py:285
  730.3 12.0 copy-start.49
  (61 other events, 180.6 us)
Sparse Core Ops, SparseCore 0:
  10.9 72.2 all-gather.7
  102.5 33.0 all-gather.11
  137.2 34.4 all-gather.9
  174.4 56.4 all-gather.13
  233.6 76.3 all-gather.15
  312.7 76.0 all-gather.17
  604.4 43.0 reduce-scatter.6
  650.2 44.5 reduce-scatter.8
  697.6 141.0 reduce-scatter.12
  845.2 151.3 reduce-scatter.10
  999.6 181.7 reduce-scatter.14
  1184.2 184.5 reduce-scatter.16
where the time goes:
time: 1380 us
  waiting for transfers between devices  808 us (59%)
  matrix products  200 us (14%)
  blocking collectives  122 us (9%)
  local copies, waits for them, and re-layouts  121 us (9%)
  other arithmetic  107 us (8%)
  between operations  15.2 us (1%)
    reduce_scatter x1, waiting for transfers between devices, per_device(): lax.psum_scatter(mlp_terms[4], ('dp', 'ctx'), scatter_dimension=0, tiled=...  187 us
    reduce_scatter x1, waiting for transfers between devices, per_device(): lax.psum_scatter(mlp_terms[2], ('dp', 'ctx'), scatter_dimension=0, tiled=...  185 us
    reduce_scatter x1, waiting for transfers between devices, per_device(): lax.psum_scatter(attn_terms[2], ('dp', 'ctx'), scatter_dimension=0, tiled...  158 us
    unnamed x2, blocking collectives  83.3 us
    all_gather x1, waiting for transfers between devices, per_device(): lax.all_gather(up_weight, ('dp', 'ctx'), axis=0, tiled=True)  69.7 us
    all_gather x1, waiting for transfers between devices, per_device(): lax.all_gather(down_weight, ('dp', 'ctx'), axis=0, tiled=True)  68.5 us
    dot_general x16, matrix products, head_scores(): jnp.einsum('qhd,khd->hqk', q_heads, k_heads, preferred_element_type=jnp.f...  52.6 us
    convert_element_type x8, other arithmetic, backward_block(): grad_scores = (probs * (grad_probs - inner)).astype(jnp.bfloat16)  52.5 us
  transfers between devices with their start and end apart: 12, of which 10 were waited for; matrix products, arithmetic and copies ran while one was open for 14% of the time, Pallas kernels for 0%

commit v1 on v0

v1 whole, which is shorter than its diff:
```python
import math

import jax
import jax.numpy as jnp
from jax import lax
from jax.experimental import pallas as pl
from jax.experimental.pallas import tpu as pltpu
from jax.sharding import Mesh
from jax.sharding import PartitionSpec as P

D = 1024
HD = 64
GAP = HD // 6
EPSILON = 1e-06
BF = jnp.bfloat16
F32 = jnp.float32
ALL = ("o", "y", "x", "c")
SWAP = ((0, 1), (1, 0))
DIAGONAL = ((0, 3), (1, 2), (2, 1), (3, 0))
NT = (((1,), (1,)), ((), ()))
NN = (((1,), (0,)), ((), ()))
TN = (((0,), (0,)), ((), ()))
VMEM_LIMIT = 50 * 2**20


def dot(left, right, dims=NN):
    return lax.dot_general(left, right, dims, preferred_element_type=F32)


def swap(values, axis):
    return lax.ppermute(values, axis, SWAP)


def by_place(flag, own, other):
    return jnp.where(flag == 0, own, other), jnp.where(flag == 0, other, own)


def place_four(high, low, parts):
    first = by_place(low, parts[0], parts[1])
    second = by_place(low, parts[2], parts[3])
    even = by_place(high, first[0], second[0])
    odd = by_place(high, first[1], second[1])
    return even[0], odd[0], even[1], odd[1]


def norm_parts(values):
    average = jnp.mean(values, axis=-1, keepdims=True)
    centred = values - average
    spread = jnp.mean(centred * centred, axis=-1, keepdims=True)
    scale = lax.rsqrt(spread + EPSILON)
    return centred * scale, scale


def norm_back(unit, scale, grad, gain):
    scaled = grad * gain
    return scale * (
        scaled
        - jnp.mean(scaled, axis=-1, keepdims=True)
        - unit * jnp.mean(scaled * unit, axis=-1, keepdims=True)
    )


def rotary_tables(places, width):
    column = jnp.arange(width) % HD
    segment = column // (2 * GAP)
    within = column % (2 * GAP)
    freq_index = (within % GAP).astype(F32)
    frequency = jnp.power(10000.0, -freq_index / GAP)
    angles = jnp.zeros((places.shape[1], width), F32)
    for axis_num in range(3):
        angles = (
            angles
            + places[axis_num][:, None] * jnp.where(segment == axis_num, frequency, 0.0)[None, :]
        )
    rotated = segment < 3
    cosine = jnp.where(rotated, jnp.cos(angles), 1.0)
    sine = jnp.where(rotated, jnp.sin(angles), 0.0)
    return cosine, sine, within < GAP


def partner_of(values, leading):
    return jnp.where(leading, -jnp.roll(values, -GAP, axis=1), jnp.roll(values, GAP, axis=1))


def attend_kernel(q_ref, k_ref, v_ref, o_ref, wide_ref, lse_ref):
    q, k, v = q_ref[...], k_ref[...], v_ref[...]
    lane = lax.broadcasted_iota(jnp.int32, (1, 2 * HD), 1)
    mixed, logs = [], []
    for head in range(2):
        mine = (lane < HD) if head == 0 else (lane >= HD)
        scores = dot(jnp.where(mine, q, 0), k, NT)
        top = jnp.max(scores, axis=1, keepdims=True)
        weight = jnp.exp(scores - top)
        total = jnp.sum(weight, axis=1, keepdims=True)
        mixed.append(dot(weight.astype(BF), v) / total)
        logs.append(top + jnp.log(total))
    out = jnp.where(lane < HD, mixed[0], mixed[1])
    o_ref[...] = out.astype(BF)
    wide_ref[...] = out
    lse_ref[...] = jnp.where(lane < HD, logs[0], logs[1])


def attend(q, k, v, rows=256):
    count, width = q.shape
    part = pl.BlockSpec((rows, 2 * HD), lambda pair, i: (i, pair))
    full = pl.BlockSpec((count, 2 * HD), lambda pair, i: (0, pair))
    return pl.pallas_call(
        attend_kernel,
        grid=(width // (2 * HD), count // rows),
        in_specs=[part, full, full],
        out_specs=[part, part, part],
        out_shape=[
            jax.ShapeDtypeStruct(q.shape, BF),
            jax.ShapeDtypeStruct(q.shape, F32),
            jax.ShapeDtypeStruct(q.shape, F32),
        ],
        compiler_params=pltpu.CompilerParams(vmem_limit_bytes=VMEM_LIMIT),
        cost_estimate=pl.CostEstimate(
            flops=35 * 10**9, bytes_accessed=8 * 2**20, transcendentals=count * count * 4
        ),
        name="attend",
    )(q, k, v)


def attend_back_kernel(
    q_ref, go_ref, wide_ref, lse_ref, k_ref, v_ref, gq_ref, gk_ref, gv_ref
):
    @pl.when(pl.program_id(1) == 0)
    def _():
        gk_ref[...] = jnp.zeros_like(gk_ref)
        gv_ref[...] = jnp.zeros_like(gv_ref)

    q, go, k, v, lse = q_ref[...], go_ref[...], k_ref[...], v_ref[...], lse_ref[...]
    lane = lax.broadcasted_iota(jnp.int32, (1, 2 * HD), 1)
    product = go.astype(F32) * wide_ref[...]
    grads = []
    for head in range(2):
        mine = (lane < HD) if head == 0 else (lane >= HD)
        q_head, go_head = jnp.where(mine, q, 0), jnp.where(mine, go, 0)
        inner = jnp.sum(jnp.where(mine, product, 0.0), axis=1, keepdims=True)
        weight = jnp.exp(dot(q_head, k, NT) - lse[:, HD * head : HD * head + 1])
        pull = (weight * (dot(go_head, v, NT) - inner)).astype(BF)
        grads.append(dot(pull, k))
        gk_ref[...] += dot(q_head.T, pull)
        gv_ref[...] += dot(go_head.T, weight.astype(BF))
    gq_ref[...] = jnp.where(lane < HD, grads[0], grads[1])


def attend_back(q, k, v, go, wide, lse, rows=256):
    count, width = q.shape
    part = pl.BlockSpec((rows, 2 * HD), lambda pair, i: (i, pair))
    full = pl.BlockSpec((count, 2 * HD), lambda pair, i: (0, pair))
    turned = pl.BlockSpec((2 * HD, count), lambda pair, i: (pair, 0))
    return pl.pallas_call(
        attend_back_kernel,
        grid=(width // (2 * HD), count // rows),
        in_specs=[part, part, part, part, full, full],
        out_specs=[part, turned, turned],
        out_shape=[
            jax.ShapeDtypeStruct(q.shape, F32),
            jax.ShapeDtypeStruct((width, count), F32),
            jax.ShapeDtypeStruct((width, count), F32),
        ],
        compiler_params=pltpu.CompilerParams(vmem_limit_bytes=VMEM_LIMIT),
        cost_estimate=pl.CostEstimate(
            flops=50 * 10**9, bytes_accessed=12 * 2**20, transcendentals=count * count * 4
        ),
        name="attend_back",
    )(q, go, wide, lse, k, v)


def per_device(
    tokens,
    positions,
    ln1_gain,
    ln1_shift,
    qkv_weight,
    qkv_bias,
    out_weight,
    out_bias,
    ln2_gain,
    ln2_shift,
    up_weight,
    up_bias,
    down_weight,
    down_bias,
    cotangent,
):
    rows = tokens.shape[0]
    outer = lax.axis_size("o")
    y, x, c = lax.axis_index("y"), lax.axis_index("x"), lax.axis_index("c")
    ctx = 2 * x + c
    shard = ln1_gain.shape[0]
    blocks = D // shard
    half_blocks = blocks // 2
    tall = up_bias.shape[0]
    ff = tall * blocks
    ff_half = ff // 2
    scaling = 1.0 / math.sqrt(HD)
    group = D // 4

    place_rows = jnp.zeros((16, D), BF).at[:3, :rows].set(positions.astype(BF))
    sent = jnp.concatenate([tokens, place_rows], axis=0)
    from_x = swap(sent, "x")
    from_c = swap(jnp.stack([sent, from_x]), "c")
    clip_rows = jnp.concatenate(
        [tokens, from_c[0, :rows], from_x[:rows], from_c[1, :rows]], axis=0
    )
    places = jnp.concatenate(
        [
            positions.astype(F32),
            from_c[0, rows : rows + 3, :rows].astype(F32),
            from_x[rows : rows + 3, :rows].astype(F32),
            from_c[1, rows : rows + 3, :rows].astype(F32),
        ],
        axis=1,
    )
    cotangent_pair = jnp.concatenate([cotangent, swap(cotangent, "c")], axis=0)

    columns = jnp.concatenate(
        [
            ln1_gain[None],
            ln1_shift[None],
            qkv_bias.reshape(3, shard),
            out_bias[None],
            ln2_gain[None],
            ln2_shift[None],
            up_bias.reshape(-1, shard),
            down_bias[None],
        ],
        axis=0,
    )
    n_vectors = columns.shape[0]
    columns = jnp.pad(columns, ((0, 128 - n_vectors), (0, 0))).T
    packed = qkv_weight.reshape(shard, 3, 4, group).transpose(2, 0, 1, 3).reshape(4, shard, -1)
    packed = jnp.concatenate([packed, jnp.broadcast_to(columns, (4, shard, 128))], axis=2)
    packed = lax.all_to_all(packed, ("x", "c"), 0, 0, tiled=True)
    gathered = lax.all_gather(
        packed.reshape(4 * shard, -1), ("o", "y"), axis=0, tiled=True
    )
    qkv_full = gathered[:, : 3 * group]
    vectors = gathered[:, 3 * group : 3 * group + n_vectors].astype(F32).T
    gain_one, shift_one = vectors[0], vectors[1]
    bias_qkv = vectors[2:5].reshape(3, blocks, shard).transpose(1, 0, 2).reshape(3, 4, group)
    bias_qkv = lax.dynamic_index_in_dim(bias_qkv, ctx, 1, keepdims=False).reshape(-1)
    bias_out, gain_two, shift_two = vectors[5], vectors[6], vectors[7]
    bias_up = vectors[8:-1].reshape(-1, blocks, shard).transpose(1, 0, 2)
    bias_up = lax.dynamic_index_in_dim(
        bias_up.reshape(half_blocks, 2, tall), c, 1, keepdims=False
    ).reshape(-1)
    bias_down = vectors[-1]

    up_parts = up_weight.reshape(shard, half_blocks, 2, tall)
    out_parts = out_weight.reshape(shard, 2, D // 2)

    def column_half(which):
        return jnp.concatenate(
            [
                lax.dynamic_index_in_dim(up_parts, which, 2, keepdims=False).reshape(shard, -1),
                lax.dynamic_index_in_dim(out_parts, which, 1, keepdims=False),
            ],
            axis=1,
        )

    upper = jnp.concatenate(by_place(c, column_half(c), swap(column_half(1 - c), "c")), axis=0)
    upper = lax.all_gather(upper, "o", axis=0, tiled=False)
    upper_x = swap(upper, "x")
    upper_y = swap(upper, "y")
    upper_xy = swap(upper_x, "y")
    upper = jnp.stack(place_four(y, x, (upper, upper_x, upper_y, upper_xy)), axis=1)
    upper = upper.reshape(D, -1)
    up_half = upper[:, :ff_half]
    out_half = upper[:, ff_half:]
    out_full = jnp.concatenate(by_place(c, out_half, swap(out_half, "c")), axis=1)
    lower = lax.all_gather(down_weight, "o", axis=0, tiled=False)
    lower_y = swap(lower, "y")
    lower_x = swap(lower, "x")
    lower_xy = swap(lower_y, "x")
    lower = jnp.stack(place_four(y, x, (lower, lower_x, lower_y, lower_xy)), axis=1)
    down_half = lower.reshape(ff_half, D)

    inputs_f = tokens.astype(F32)
    clip_unit, _ = norm_parts(clip_rows.astype(F32))
    normed_low = (clip_unit * gain_one + shift_one).astype(BF)
    joined = dot(normed_low, qkv_full) + bias_qkv
    cosine, sine, leading = rotary_tables(places, 2 * HD)
    cosine, sine = jnp.tile(cosine, (1, 2)), jnp.tile(sine, (1, 2))
    leading = jnp.tile(leading, 2)

    def turn(part):
        return part * cosine + partner_of(part, leading) * sine

    queries = (turn(joined[:, :group]) * scaling).astype(BF)
    keys_low = turn(joined[:, group : 2 * group]).astype(BF)
    values_low = joined[:, 2 * group :].astype(BF)
    mixed, mixed_wide, row_logs = attend(queries, keys_low, values_low)

    def to_owners(values):
        parts = (
            values[:rows],
            swap(values[rows : 2 * rows], "c"),
            swap(values[2 * rows : 3 * rows], "x"),
            lax.ppermute(values[3 * rows :], ("x", "c"), DIAGONAL),
        )
        return jnp.concatenate(place_four(x, c, parts), axis=1)

    mixed_low = to_owners(mixed)
    attn_out = dot(mixed_low, out_full) + bias_out
    middle = inputs_f + attn_out
    unit_two, scale_two = norm_parts(middle)
    normed_two = (unit_two * gain_two + shift_two).astype(BF)

    normed_pair = jnp.concatenate([normed_two, swap(normed_two, "c")], axis=0)
    upward = dot(normed_pair, up_half) + bias_up
    bell = 0.5 * (1.0 + lax.erf(upward * 0.7071067811865476))
    active = (upward * bell).astype(BF)
    mlp_part = dot(active, down_half)
    grad_active = dot(cotangent_pair, down_half, NT)
    slope = bell + upward * jnp.exp(-0.5 * upward * upward) * (1.0 / math.sqrt(2.0 * math.pi))
    grad_up = (grad_active * slope).astype(BF)
    down_grad = dot(active, cotangent_pair, TN).astype(BF)
    up_grad = dot(normed_pair, grad_up, TN).astype(BF)
    up_bias_grad = jnp.sum(grad_up.astype(F32), axis=0)
    grad_two = dot(grad_up, up_half, NT)
    grad_two = grad_two[:rows] + swap(grad_two[rows:], "c")
    mlp_out = mlp_part[:rows] + swap(mlp_part[rows:], "c") + bias_down
    final_out = middle + mlp_out
    squares = jnp.stack(
        [
            jnp.sum(inputs_f * inputs_f),
            jnp.sum(attn_out * attn_out),
            jnp.sum(middle * middle),
            jnp.sum(mlp_out * mlp_out),
            jnp.sum(final_out * final_out),
        ]
    )
    squares = jnp.pad(squares[None], ((0, 7), (0, 123)))
    squares = lax.all_gather(squares, ALL, axis=0, tiled=False)
    entry_count = rows * lax.axis_size(ALL) * D
    norm_stats = jnp.sqrt(jnp.sum(squares[:, 0, :5], axis=0) / entry_count)

    grad_final = cotangent.astype(F32)
    down_bias_grad = jnp.sum(grad_final, axis=0)
    gain_two_grad = jnp.sum(grad_two * unit_two, axis=0)
    shift_two_grad = jnp.sum(grad_two, axis=0)
    grad_middle = grad_final + norm_back(unit_two, scale_two, grad_two, gain_two)
    grad_attn = grad_middle.astype(BF)
    out_bias_grad = jnp.sum(grad_attn.astype(F32), axis=0)
    out_grad = dot(mixed_low, grad_attn, TN).astype(BF).reshape(D, 2, D // 2)
    out_grad = lax.dynamic_index_in_dim(out_grad, c, 1, keepdims=False) + swap(
        lax.dynamic_index_in_dim(out_grad, 1 - c, 1, keepdims=False), "c"
    )
    grad_mixed = dot(grad_attn, out_full, NT).astype(BF)

    grad_groups = grad_mixed.reshape(rows, 4, group)

    def group_of(place):
        return lax.dynamic_index_in_dim(grad_groups, ctx ^ place, 1, keepdims=False)

    grad_mixed = jnp.concatenate(
        [
            group_of(0),
            swap(group_of(1), "c"),
            swap(group_of(2), "x"),
            lax.ppermute(group_of(3), ("x", "c"), DIAGONAL),
        ],
        axis=0,
    )

    def to_column(values, first, second):
        parts = values.reshape(outer, 2, 2, -1, values.shape[-1])
        flags = {"y": y, "x": x}

        def quarter(flip_first, flip_second):
            flips = {first: flip_first, second: flip_second}
            place = (flags["y"] ^ flips["y"]) * 2 + (flags["x"] ^ flips["x"])
            return lax.dynamic_index_in_dim(
                parts.reshape(outer, 4, -1, values.shape[-1]), place, 1, keepdims=False
            )

        passed = swap(quarter(1, 1), first)
        kept = swap(quarter(1, 0), first)
        passed = swap(quarter(0, 1) + passed, second)
        summed = quarter(0, 0) + kept + passed
        return lax.psum_scatter(summed, "o", scatter_dimension=0, tiled=False)

    down_weight_grad = to_column(down_grad, "x", "y").astype(F32)
    upper_grad = to_column(jnp.concatenate([up_grad, out_grad], axis=1), "y", "x")
    upper_grad = upper_grad.reshape(2, shard, -1)
    upper_own = lax.dynamic_index_in_dim(upper_grad, c, 0, keepdims=False)
    upper_other = swap(lax.dynamic_index_in_dim(upper_grad, 1 - c, 0, keepdims=False), "c")
    upper_even, upper_odd = by_place(c, upper_own.astype(F32), upper_other.astype(F32))
    up_weight_grad = jnp.stack(
        [
            upper_even[:, :ff_half].reshape(shard, half_blocks, tall),
            upper_odd[:, :ff_half].reshape(shard, half_blocks, tall),
        ],
        axis=2,
    ).reshape(shard, ff)
    out_weight_grad = jnp.concatenate([upper_even[:, ff_half:], upper_odd[:, ff_half:]], axis=1)

    grad_q, grad_k, grad_v = attend_back(
        queries, keys_low, values_low, grad_mixed, mixed_wide, row_logs
    )

    def turn_back(grad):
        return grad * cosine - partner_of(grad * sine, leading)

    grad_joined = jnp.concatenate(
        [turn_back(grad_q) * scaling, turn_back(grad_k.T), grad_v.T], axis=1
    ).astype(BF)
    qkv_grad = dot(normed_low, grad_joined, TN)
    qkv_bias_grad = jnp.sum(grad_joined.astype(F32), axis=0)
    grad_normed = dot(grad_joined, qkv_full, NT)

    grad_parts = grad_normed.reshape(4, rows, D)
    to_core = swap(grad_parts[1::2].astype(BF), "c").astype(F32)
    own_part = grad_parts[0] + to_core[0]
    grad_one = own_part + swap((grad_parts[2] + to_core[1]).astype(BF), "x").astype(F32)
    unit_one, scale_one = norm_parts(inputs_f)
    input_grad = grad_middle + norm_back(unit_one, scale_one, grad_one, gain_one)
    gain_one_grad = jnp.sum(grad_one * unit_one, axis=0)
    shift_one_grad = jnp.sum(grad_one, axis=0)

    mine = (jnp.arange(4) == ctx)[None, :, None]
    qkv_bias_grad = jnp.where(mine, qkv_bias_grad.reshape(3, 1, group), 0.0)
    qkv_bias_grad = qkv_bias_grad.reshape(blocks, 3, shard).transpose(1, 0, 2).reshape(3, D)
    mine = (jnp.arange(2) == c)[None, :, None]
    up_bias_grad = jnp.where(mine, up_bias_grad.reshape(half_blocks, 1, tall), 0.0)
    up_bias_grad = up_bias_grad.reshape(blocks, -1, shard).transpose(1, 0, 2).reshape(-1, D)
    vector_grads = jnp.concatenate(
        [
            gain_one_grad[None],
            shift_one_grad[None],
            qkv_bias_grad,
            out_bias_grad[None],
            gain_two_grad[None],
            shift_two_grad[None],
            up_bias_grad,
            down_bias_grad[None],
        ],
        axis=0,
    )
    vector_grads = jnp.pad(vector_grads, ((0, 128 - n_vectors), (0, 0))).T
    last = jnp.concatenate([qkv_grad, vector_grads], axis=1).astype(BF)
    last = last.reshape(outer, 2, 4 * shard, -1)
    last = lax.dynamic_index_in_dim(last, y, 1, keepdims=False) + swap(
        lax.dynamic_index_in_dim(last, 1 - y, 1, keepdims=False), "y"
    )
    last = lax.psum_scatter(last, "o", scatter_dimension=0, tiled=False)
    last = lax.all_to_all(last.reshape(4, shard, -1), ("x", "c"), 0, 0, tiled=True)
    last = last.astype(F32)
    qkv_weight_grad = (
        last[:, :, : 3 * group].reshape(4, shard, 3, group).transpose(1, 2, 0, 3)
    ).reshape(shard, 3 * D)
    vector_grads = jnp.sum(last[:, :, 3 * group : 3 * group + n_vectors], axis=0).T

    return (
        final_out.astype(BF),
        input_grad,
        vector_grads[0],
        vector_grads[1],
        qkv_weight_grad,
        vector_grads[2:5].reshape(-1),
        out_weight_grad,
        vector_grads[5],
        vector_grads[6],
        vector_grads[7],
        up_weight_grad,
        vector_grads[8:-1].reshape(-1),
        down_weight_grad,
        vector_grads[-1],
        norm_stats,
    )


def solution(mesh):
    devices = mesh.devices
    fine = Mesh(devices.reshape(-1, 2, 2, 2), ALL)
    rows, vector, whole = P(ALL, None), P(ALL), P()
    in_specs = (
        rows,
        P(None, ALL),
        vector,
        vector,
        rows,
        vector,
        rows,
        vector,
        vector,
        vector,
        rows,
        vector,
        rows,
        vector,
        rows,
    )
    out_specs = (
        rows,
        rows,
        vector,
        vector,
        rows,
        vector,
        rows,
        vector,
        vector,
        vector,
        rows,
        vector,
        rows,
        vector,
        whole,
    )
    return jax.shard_map(
        per_device, mesh=fine, in_specs=in_specs, out_specs=out_specs, check_vma=False
    )
```

time: 1380 us -> 638 us (0.46)
  waiting for transfers between devices: 808 us -> 232 us
  matrix products: 200 us -> 66.3 us
  blocking collectives: 122 us -> 38.7 us
  Pallas kernels: 0 us -> 75.7 us
  local copies, waits for them, and re-layouts: 121 us -> 80.1 us
  starting transfers between devices: 0.48 us -> 33.1 us
  other arithmetic: 107 us -> 91 us
    reduce_scatter x6 -> x3, waiting for transfers between devices: 626 us -> 0.02 us  [the longest x2 0.02 us: to_column(): return lax.psum_scatter(summed, 'o', scatter_dimension=0, tiled=False)]
    ppermute x0 -> x31, waiting for transfers between devices: none -> 167 us  [the longest x29 164 us: swap(): return lax.ppermute(values, axis, SWAP)]
    dot_general x68 -> x12, matrix products: 200 us -> 66.3 us  [dot(): return lax.dot_general(left, right, dims, preferred_element_type=F32)]
    all_gather x6 -> x3, waiting for transfers between devices: 180 us -> 57.4 us  [the longest x1 39.7 us: per_device(): lax.all_gather(packed.reshape(4 * shard, -1), ('o', 'y'), axis=0, tiled=T...]
    unnamed x2 -> x0, blocking collectives: 83.3 us -> none
    pallas_call x0 -> x2, Pallas kernels: none -> 75.7 us  [the longest x1 44 us: attend_back(): pl.pallas_call(attend_back_kernel, grid=(width // (2 * HD), count // rows...]
    convert_element_type x18 -> x10, other arithmetic: 63.8 us -> 14.8 us  [the longest x1 4.41 us: per_device(): (grad_parts[2] + to_core[1]).astype(BF)]
    dynamic_slice x40 -> x6, local copies, waits for them, and re-layouts: 36 us -> 6.17 us  [the longest x1 2.96 us: group_of(): return lax.dynamic_index_in_dim(grad_groups, ctx ^ place, 1, keepdims=False)]
  transfers between devices with their start and end apart: 12 -> 39, of which waited for: 10 -> 17; matrix products, arithmetic and copies ran while one was open for 14% -> 31% of each run, Pallas kernels for 0% -> 12%
where the time goes in v1:
time: 638 us; the launch traced here: 633 us
  waiting for transfers between devices  232 us (36%)
  other arithmetic  91 us (14%)
  local copies, waits for them, and re-layouts  80.1 us (13%)
  Pallas kernels  75.7 us (12%)
  matrix products  66.3 us (10%)
  blocking collectives  38.7 us (6%)
  starting transfers between devices  33.1 us (5%)
  between operations  16 us (3%)
    ppermute x29, waiting for transfers between devices, swap(): return lax.ppermute(values, axis, SWAP)  164 us
    dot_general x12, matrix products, dot(): return lax.dot_general(left, right, dims, preferred_element_type=F32)  66.3 us
    pallas_call x1, Pallas kernels, attend_back(): pl.pallas_call(attend_back_kernel, grid=(width // (2 * HD), count // rows...  44 us
    all_gather x1, waiting for transfers between devices, per_device(): lax.all_gather(packed.reshape(4 * shard, -1), ('o', 'y'), axis=0, tiled=T...  39.7 us
    all_gather x1, blocking collectives, per_device(): squares = lax.all_gather(squares, ALL, axis=0, tiled=False)  38.7 us
    pallas_call x1, Pallas kernels, attend(): pl.pallas_call(attend_kernel, grid=(width // (2 * HD), count // rows), in...  31.7 us
    ppermute x29, starting transfers between devices, swap(): return lax.ppermute(values, axis, SWAP)  26 us
    unnamed x189, local copies, waits for them, and re-layouts  22.3 us
  transfers between devices with their start and end apart: 39, of which 17 were waited for; matrix products, arithmetic and copies ran while one was open for 31% of the time, Pallas kernels for 12%

profile of v1, /device:TPU:0, one launch (start us, length us, event | category | flops | bytes accessed | tf_op | source)
XLA Modules:
  0.0 633.1 jit_solution(11210706961402137462)
XLA Ops:
  18.4 22.9 %collective-permute-done = bf16[528,1024]{1,0:T(8,128)(2,1)S(1)} collective-permute-done((bf16[528,1024]{1,0:T(8,128)(2,1)}, bf16[528,1024]{1,0:T(8,128)(2,1)S(1)}, u32[]{:S(2)}, u32[]{:S(2)}) %collective-permute-start) | collective-permute-done | bytes 1081376 | tf_op jit(solution)/shard_map/ppermute | solution.py:31
  44.6 3.4 all-to-all-start
  57.0 17.6 %all-gather.9.cloned.1.call-done = bf16[256,2560]{1,0:T(8,128)(2,1)} async-done(((bf16[64,2560]{1,0:T(8,128)(2,1)}), bf16[256,2560]{1,0:T(8,128)(2,1)}) %all-gather.9.cloned.1.call-update) | async-done | bytes 1310736 | tf_op jit(solution)/shard_map/all_gather | solution.py:266
  80.3 3.5 fusion.2
  84.6 5.8 cosine_select_fusion
  90.4 39.7 %all-gather.7.cloned.1.call-done = bf16[1024,896]{0,1:T(8,128)(2,1)} async-done(((bf16[128,896]{0,1:T(8,128)(2,1)}), bf16[1024,896]{0,1:T(8,128)(2,1)}) %all-gather.7.cloned.1.call-update) | async-done | bytes 1835024 | tf_op jit(solution)/shard_map/all_gather | solution.py:238
  131.8 6.0 convolution_add_fusion
  139.4 3.4 fusion.82
  151.7 16.8 %collective-permute-done.8 = bf16[4,64,2560]{2,1,0:T(8,128)(2,1)S(1)} collective-permute-done((bf16[4,64,2560]{2,1,0:T(8,128)(2,1)}, bf16[4,64,2560]{2,1,0:T(8,128)(2,1)S(1)}, u32[]{:S(2)}, u32[]{:S(2)}) %collective-permute-start.8) | collective-permute-done | bytes 1310752 | tf_op jit(solution)/shard_map/ppermute | solution.py:31
  174.7 31.7 %attend.1 = (bf16[2048,256]{1,0:T(8,128)(2,1)S(1)}, f32[2048,256]{1,0:T(8,128)}, f32[2048,256]{1,0:T(8,128)}) custom-call(bf16[2048,256]{1,0:T(8,128)(2,1)S(1)} %get-tuple-element.70.q_ref, bf16[2048,256]{1,0:T(8,128)(2,1)S(1)} %get-tuple-element.69.k_ref, bf16[2048,256]{1,0:T(8,128)(2,1)} %slice.427.v_ref), custom_call_target="tpu_custom_call" | custom-call | flops 35000000512 | bytes 8388608 | tf_op jit(solution)/shard_map/attend/pallas_call | solution.py:107
  213.2 3.6 collective-permute-done.3
  217.3 3.1 collective-permute-done.4
  229.2 15.5 %collective-permute-done.11 = bf16[4,128,1024]{2,1,0:T(8,128)(2,1)S(1)} collective-permute-done((bf16[4,128,1024]{2,1,0:T(8,128)(2,1)}, bf16[4,128,1024]{2,1,0:T(8,128)(2,1)S(1)}, u32[]{:S(2)}, u32[]{:S(2)}) %collective-permute-start.11) | collective-permute-done | bytes 1048608 | tf_op jit(solution)/shard_map/ppermute | solution.py:31
  244.7 20.4 %collective-permute-done.13 = bf16[4,128,1024]{2,1,0:T(8,128)(2,1)S(1)} collective-permute-done((bf16[4,128,1024]{2,1,0:T(8,128)(2,1)}, bf16[4,128,1024]{2,1,0:T(8,128)(2,1)S(1)}, u32[]{:S(2)}, u32[]{:S(2)}) %collective-permute-start.13) | collective-permute-done | bytes 1048608 | tf_op jit(solution)/shard_map/ppermute | solution.py:31
  268.3 7.0 %multiply_convert_fusion = (bf16[1024,2048]{1,0:T(8,128)(2,1)}, f32[1024,2048]{1,0:T(8,128)S(1)}) fusion(f32[2048]{0:T(1024)S(1)} %bitcast.317, bf16[1024,2560]{1,0:T(8,128)(2,1)S(1)} %bitcast.256, bf16[512,1024]{1,0:T(8,128)(2,1)S(1)} %collective-permute-done.10, bf16[512,1024]{1,0:T(8,128)(2,1)S(1)} %add_convert_fusion), kind=kOutput, calls=%fused_computation.16 | convolution fusion | flops 4311744512 | bytes 18882560 | tf_op jit(solution)/shard_map/dot_general | solution.py:27
  275.3 8.2 %convert_reduce_fusion.1 = (bf16[2048]{0:T(1024)(128)(2,1)S(1)}, bf16[1024,2048]{1,0:T(8,128)(2,1)S(1)}) fusion(f32[1024,2048]{1,0:T(8,128)S(1)} %get-tuple-element.147, f32[2048]{0:T(1024)S(1)} %bitcast.318, bf16[1024,1024]{1,0:T(8,128)(2,1)S(1)} %copy-done.44, bf16[2048,1024]{1,0:T(8,128)(2,1)S(1)} %bitcast.264), kind=kOutput, calls=%fused_computation.15 | convolution fusion | flops 4322228224 | bytes 18886656 | tf_op jit(solution)/shard_map/dot_general | solution.py:27
  283.6 4.5 fusion.12
  292.5 4.5 fusion.91
  299.7 7.4 %convolution_convert_fusion = bf16[2048,1024]{1,0:T(8,128)(2,1)S(1)} fusion(bf16[1024,2048]{1,0:T(8,128)(2,1)} %get-tuple-element.146, bf16[1024,1024]{1,0:T(8,128)(2,1)} %constant_dynamic-update-slice_fusion), kind=kOutput, calls=%fused_computation.23 | convolution fusion | flops 4297064448 | bytes 10485760 | tf_op jit(solution)/shard_map/dot_general | solution.py:27
  312.1 9.8 %convolution_convert_fusion.1 = bf16[1024,2048]{1,0:T(8,128)(2,1)} fusion(bf16[1024,2048]{1,0:T(8,128)(2,1)} %copy-done.83, bf16[512,1024]{1,0:T(8,128)(2,1)} %copy-done.80, bf16[512,1024]{1,0:T(8,128)(2,1)} %copy-done.43), kind=kOutput, calls=%fused_computation.24 | convolution fusion | flops 4301258752 | bytes 10485760 | tf_op jit(solution)/shard_map/dot_general | solution.py:27
  321.9 14.1 %collective-permute-done.29 = bf16[4,128,1024]{2,1,0:T(8,128)(2,1)} collective-permute-done((bf16[4,128,1024]{2,1,0:T(8,128)(2,1)}, bf16[4,128,1024]{2,1,0:T(8,128)(2,1)}, u32[]{:S(2)}, u32[]{:S(2)}) %collective-permute-start.29) | collective-permute-done | bytes 1048608 | tf_op jit(solution)/shard_map/ppermute | solution.py:31
  340.2 5.5 multiply_reduce_fusion
  345.7 2.8 convert_reduce_fusion.4
  354.0 3.0 constant_dynamic-slice_fusion.5
  359.2 4.2 collective-permute-done.30
  363.4 3.0 fusion.54
  366.5 3.5 collective-permute-done.18
  371.2 44.0 %attend_back.1 = (f32[2048,256]{1,0:T(8,128)}, f32[256,2048]{1,0:T(8,128)}, f32[256,2048]{1,0:T(8,128)}) custom-call(bf16[2048,256]{1,0:T(8,128)(2,1)S(1)} %get-tuple-element.70.q_ref, bf16[2048,256]{1,0:T(8,128)(2,1)S(1)} %pad_maximum_fusion.13.go_ref, f32[2048,256]{1,0:T(8,128)} %get-tuple-element.34.wide_ref, f32[2048,256]{1,0:T(8,128)} %get-tuple-element.35.lse_ref, ...), custom_call_target="tpu_custom_call" | custom-call | flops 49999998976 | bytes 12582912 | tf_op jit(solution)/shard_map/attend_back/pallas_call | solution.py:154
  415.3 3.0 copy.160
  422.6 2.7 fusion.84
  425.2 2.7 fusion.86
  431.9 7.0 %fusion.36 = (bf16[2048,256]{1,0:T(8,128)(2,1)S(1)}, bf16[2048,256]{1,0:T(8,128)(2,1)S(1)}) fusion(f32[2048,256]{1,0:T(8,128)} %get-tuple-element.36, f32[2048,10]{1,0:T(8,128)} %get-tuple-element.103, f32[2048,246]{1,0:T(8,128)} %get-tuple-element.105, f32[2048,246]{1,0:T(8,128)} %get-tuple-element.104, f32[2048,10]{1,0:T(8,128)} %get-tuple-element.102, ...), kind=kLoop, calls=%fused_computation.67 | loop fusion | flops 7864320 | bytes 16777472 | tf_op jit(solution)/shard_map/convert.33
  438.9 5.6 fusion.90
  455.6 7.4 %convolution_convert_fusion.3 = bf16[1024,768]{1,0:T(8,128)(2,1)} fusion(bf16[2048,256]{1,0:T(8,128)(2,1)} %bitcast.267, bf16[2048,256]{1,0:T(8,128)(2,1)} %copy-done.32, bf16[2048,256]{1,0:T(8,128)(2,1)} %copy-done.30, f32[1024]{0:T(1024)S(1)} %bitcast.320, f32[1024]{0:T(1024)S(1)} %bitcast.309, f32[2048]{0:T(1024)S(1)} %copy-done.65, ...), kind=kOutput, calls=%fused_computation.105 | convolution fusion | flops 3258712064 | bytes 8937472 | tf_op jit(solution)/shard_map/dot_general | solution.py:27
  466.4 4.4 fusion.40
  477.9 18.6 %collective-permute-done.21 = bf16[512,1024]{1,0:T(8,128)(2,1)} collective-permute-done((bf16[512,1024]{1,0:T(8,128)(2,1)}, bf16[512,1024]{1,0:T(8,128)(2,1)}, u32[]{:S(2)}, u32[]{:S(2)}) %collective-permute-start.21) | collective-permute-done | bytes 1048608 | tf_op jit(solution)/shard_map/ppermute | solution.py:31
  496.4 5.6 fusion.26
  505.3 3.1 collective-permute-done.25
  508.5 2.9 bitcast_add_fusion
  511.4 16.7 %collective-permute-done.22 = bf16[4,128,896]{2,1,0:T(8,128)(2,1)} collective-permute-done((bf16[4,128,896]{2,1,0:T(8,128)(2,1)}, bf16[4,128,896]{2,1,0:T(8,128)(2,1)}, u32[]{:S(2)}, u32[]{:S(2)}) %collective-permute-start.22) | collective-permute-done | bytes 917536 | tf_op jit(solution)/shard_map/ppermute | solution.py:31
  530.5 24.9 %collective-permute-done.24 = bf16[4,64,2560]{2,1,0:T(8,128)(2,1)} collective-permute-done((bf16[4,64,2560]{2,1,0:T(8,128)(2,1)}, bf16[4,64,2560]{2,1,0:T(8,128)(2,1)}, u32[]{:S(2)}, u32[]{:S(2)}) %collective-permute-start.24) | collective-permute-done | bytes 1310752 | tf_op jit(solution)/shard_map/ppermute | solution.py:31
  555.4 3.4 fusion.52
  558.8 2.9 add_convert_fusion.1
  563.5 3.3 stack.79
  566.9 38.7 %all-gather.2 = f32[256,128]{1,0:T(8,128)S(1)} all-gather(f32[8,128]{1,0:T(8,128)S(1)} %pad.21), channel_id=4, replica_groups=mesh['o'=4,'y'=2,'x'=2,'c'=2] {'o','y','x','c'}, dimensions={0}, use_global_device_ids=true | all-gather | bytes 135168 | tf_op jit(solution)/shard_map/all_gather | solution.py:338
  606.2 4.2 fusion.25
  610.4 3.4 all-to-all-start.1
  615.3 4.2 all-to-all-done.1
  (398 shorter events, 137.5 us)
Async XLA Ops:
  7.2 48.0 %all-gather.11.cloned.1.call-start = ((), (), s32[]{:S(2)}) async-start(), calls=%async_computation.10 | async-start | bytes 1310720 | tf_op jit(solution)/shard_map/all_gather | solution.py:275
  7.9 66.7 %all-gather.9.cloned.1.call-start = ((), (), s32[]{:S(2)}) async-start(), calls=%async_computation.9 | async-start | bytes 1638400 | tf_op jit(solution)/shard_map/all_gather | solution.py:266
  12.4 4.3 collective-permute-start.5
  14.1 27.2 %collective-permute-start = (bf16[528,1024]{1,0:T(8,128)(2,1)}, bf16[528,1024]{1,0:T(8,128)(2,1)S(1)}, u32[]{:S(2)}, u32[]{:S(2)}) collective-permute-start(bf16[528,1024]{1,0:T(8,128)(2,1)} %get-tuple-element.117), channel_id=1, source_target_pairs={{0,2},{2,0},{1,3},{3,1},{4,6},{6,4},{5,7},{7,5},{8,10},{10,8},{9,1... | collective-permute-start | bytes 3244040 | tf_op jit(solution)/shard_map/ppermute | solution.py:31
  43.0 34.6 %collective-permute-start.1 = (bf16[2,528,1024]{2,1,0:T(8,128)(2,1)}, bf16[2,528,1024]{2,1,0:T(8,128)(2,1)}, u32[]{:S(2)}, u32[]{:S(2)}) collective-permute-start(bf16[2,528,1024]{2,1,0:T(8,128)(2,1)} %pad_maximum_fusion.5), channel_id=1, source_target_pairs={{0,1},{1,0},{2,3},{3,2},{4,5},{5,4},{6,7},{7,6},{8,9},{9,8},{10,11... | collective-permute-start | bytes 6488072 | tf_op jit(solution)/shard_map/ppermute | solution.py:31
  44.6 9.1 %all-to-all-start = ((bf16[4,32,896]{2,1,0:T(8,128)(2,1)}), bf16[4,32,896]{2,1,0:T(8,128)(2,1)S(1)}, u32[]{:S(2)}, u32[]{:S(2)}) async-start(bf16[4,32,896]{2,1,0:T(8,128)(2,1)} %pad_maximum_fusion.16), calls=%async_computation | async-start | bytes 458752 | tf_op jit(solution)/shard_map/all_to_all | solution.py:237
  48.0 82.2 %all-gather.7.cloned.1.call-start = ((), (), s32[]{:S(2)}) async-start(), calls=%async_computation.5 | async-start | bytes 2064384 | tf_op jit(solution)/shard_map/all_gather | solution.py:238
  48.0 159.7 %collective-permute-start.15 = (bf16[512,1024]{1,0:T(8,128)(2,1)}, bf16[512,1024]{1,0:T(8,128)(2,1)}, u32[]{:S(2)}, u32[]{:S(2)}) collective-permute-start(bf16[512,1024]{1,0:T(8,128)(2,1)} %param.31), channel_id=1, source_target_pairs={{0,1},{1,0},{2,3},{3,2},{4,5},{5,4},{6,7},{7,6},{8,9},{9,8},{10,11... | collective-permute-start | bytes 3145736 | tf_op jit(solution)/shard_map/ppermute | solution.py:31
  51.0 95.7 %copy-start.69 = (pred[256]{0:T(512)(128)(4,1)}, pred[256]{0:T(512)(128)(4,1)S(1)}, u32[]{:S(2)}) copy-start(pred[256]{0:T(512)(128)(4,1)S(1)} %broadcast_bitcast_fusion) | copy-start | bytes 772
  54.6 507.1 %reduce-scatter.8.cloned.1.call-start = ((), (), s32[]{:S(2)}) async-start(), calls=%async_computation.8 | async-start | bytes 1310720 | tf_op jit(solution)/shard_map/reduce_scatter | solution.py:385
  55.1 168.6 %copy-start.60 = (f32[512]{0:T(512)}, f32[512]{0:T(512)S(1)}, u32[]{:S(2)}) copy-start(f32[512]{0:T(512)S(1)} %broadcast_multiply_fusion.3) | copy-start | bytes 6148
  55.2 76.6 %copy-start.13 = (bf16[512,1024]{1,0:T(8,128)(2,1)}, bf16[512,1024]{1,0:T(8,128)(2,1)S(1)}, u32[]{:S(2)}) copy-start(bf16[512,1024]{1,0:T(8,128)(2,1)S(1)} %slice.309) | copy-start | bytes 3145732
  55.3 157.3 %collective-permute-start.12 = (bf16[4,128,1024]{2,1,0:T(8,128)(2,1)}, bf16[4,128,1024]{2,1,0:T(8,128)(2,1)}, u32[]{:S(2)}, u32[]{:S(2)}) collective-permute-start(bf16[4,128,1024]{2,1,0:T(8,128)(2,1)} %bitcast.279), channel_id=1, source_target_pairs={{0,4},{4,0},{1,5},{5,1},{2,6},{6,2},{3,7},{7,3},{8,12},{12,8},{9,1... | collective-permute-start | bytes 3145736 | tf_op jit(solution)/shard_map/ppermute | solution.py:31
  74.6 63.2 %collective-permute-start.6 = (bf16[4,64,2560]{2,1,0:T(8,128)(2,1)}, bf16[4,64,2560]{2,1,0:T(8,128)(2,1)}, u32[]{:S(2)}, u32[]{:S(2)}) collective-permute-start(bf16[4,64,2560]{2,1,0:T(8,128)(2,1)} %bitcast.276), channel_id=1, source_target_pairs={{0,2},{2,0},{1,3},{3,1},{4,6},{6,4},{5,7},{7,5},{8,10},{10,8},{9,1... | collective-permute-start | bytes 3932168 | tf_op jit(solution)/shard_map/ppermute | solution.py:31
  76.1 75.5 %collective-permute-start.7 = (bf16[4,64,2560]{2,1,0:T(8,128)(2,1)}, bf16[4,64,2560]{2,1,0:T(8,128)(2,1)}, u32[]{:S(2)}, u32[]{:S(2)}) collective-permute-start(bf16[4,64,2560]{2,1,0:T(8,128)(2,1)} %bitcast.277), channel_id=1, source_target_pairs={{0,4},{4,0},{1,5},{5,1},{2,6},{6,2},{3,7},{7,3},{8,12},{12,8},{9,1... | collective-permute-start | bytes 3932168 | tf_op jit(solution)/shard_map/ppermute | solution.py:31
  79.3 52.5 %copy-start.15 = (bf16[512,1024]{1,0:T(8,128)(2,1)}, bf16[512,1024]{1,0:T(8,128)(2,1)S(1)}, u32[]{:S(2)}) copy-start(bf16[512,1024]{1,0:T(8,128)(2,1)S(1)} %get-tuple-element.95) | copy-start | bytes 3145732
  80.3 51.5 %copy-start.58 = (f32[2048]{0:T(1024)}, f32[2048]{0:T(1024)S(1)}, u32[]{:S(2)}) copy-start(f32[2048]{0:T(1024)S(1)} %broadcast_multiply_fusion) | copy-start | bytes 24580
  83.8 54.0 %copy-start.64 = (f32[2048]{0:T(1024)}, f32[2048]{0:T(1024)S(1)}, u32[]{:S(2)}) copy-start(f32[2048]{0:T(1024)S(1)} %add_rsqrt_fusion) | copy-start | bytes 24580
  137.8 30.6 %collective-permute-start.8 = (bf16[4,64,2560]{2,1,0:T(8,128)(2,1)}, bf16[4,64,2560]{2,1,0:T(8,128)(2,1)S(1)}, u32[]{:S(2)}, u32[]{:S(2)}) collective-permute-start(bf16[4,64,2560]{2,1,0:T(8,128)(2,1)} %collective-permute-done.6), channel_id=1, source_target_pairs={{0,4},{4,0},{1,5},{5,1},{2,6},{6,2},{3,7},{7,3},{8,12},{12,8},{9,1... | collective-permute-start | bytes 3932168 | tf_op jit(solution)/shard_map/ppermute | solution.py:31
  173.1 48.5 %collective-permute-start.9 = (bf16[1024,512]{1,0:T(8,128)(2,1)}, bf16[1024,512]{1,0:T(8,128)(2,1)}, u32[]{:S(2)}, u32[]{:S(2)}) collective-permute-start(bf16[1024,512]{1,0:T(8,128)(2,1)} %slice.330), channel_id=1, source_target_pairs={{0,1},{1,0},{2,3},{3,2},{4,5},{5,4},{6,7},{7,6},{8,9},{9,8},{10,11... | collective-permute-start | bytes 3145736 | tf_op jit(solution)/shard_map/ppermute | solution.py:31
  207.2 9.6 %collective-permute-start.3 = (bf16[512,256]{1,0:T(8,128)(2,1)}, bf16[512,256]{1,0:T(8,128)(2,1)}, u32[]{:S(2)}, u32[]{:S(2)}) collective-permute-start(bf16[512,256]{1,0:T(8,128)(2,1)} %get-tuple-element.126), channel_id=1, source_target_pairs={{0,2},{2,0},{1,3},{3,1},{4,6},{6,4},{5,7},{7,5},{8,10},{10,8},{9,1... | collective-permute-start | bytes 786440 | tf_op jit(solution)/shard_map/ppermute | solution.py:31
  207.7 12.7 %collective-permute-start.4 = (bf16[512,256]{1,0:T(8,128)(2,1)}, bf16[512,256]{1,0:T(8,128)(2,1)}, u32[]{:S(2)}, u32[]{:S(2)}) collective-permute-start(bf16[512,256]{1,0:T(8,128)(2,1)} %get-tuple-element.125), channel_id=1, source_target_pairs={{0,3},{1,2},{2,1},{3,0},{4,7},{5,6},{6,5},{7,4},{8,11},{9,10},{10,... | collective-permute-start | bytes 786440 | tf_op jit(solution)/shard_map/ppermute | solution.py:303
  207.7 12.7 %collective-permute-start.2 = (bf16[512,256]{1,0:T(8,128)(2,1)S(1)}, bf16[512,256]{1,0:T(8,128)(2,1)}, u32[]{:S(2)}, u32[]{:S(2)}) collective-permute-start(bf16[512,256]{1,0:T(8,128)(2,1)S(1)} %get-tuple-element.124), channel_id=1, source_target_pairs={{0,1},{1,0},{2,3},{3,2},{4,5},{5,4},{6,7},{7,6},{8,9},{9,8},{10,11... | collective-permute-start | bytes 786440 | tf_op jit(solution)/shard_map/ppermute | solution.py:31
  212.6 32.1 %collective-permute-start.11 = (bf16[4,128,1024]{2,1,0:T(8,128)(2,1)}, bf16[4,128,1024]{2,1,0:T(8,128)(2,1)S(1)}, u32[]{:S(2)}, u32[]{:S(2)}) collective-permute-start(bf16[4,128,1024]{2,1,0:T(8,128)(2,1)} %bitcast.280), channel_id=1, source_target_pairs={{0,2},{2,0},{1,3},{3,1},{4,6},{6,4},{5,7},{7,5},{8,10},{10,8},{9,1... | collective-permute-start | bytes 3145736 | tf_op jit(solution)/shard_map/ppermute | solution.py:31
  216.7 48.4 %collective-permute-start.13 = (bf16[4,128,1024]{2,1,0:T(8,128)(2,1)}, bf16[4,128,1024]{2,1,0:T(8,128)(2,1)S(1)}, u32[]{:S(2)}, u32[]{:S(2)}) collective-permute-start(bf16[4,128,1024]{2,1,0:T(8,128)(2,1)} %collective-permute-done.12), channel_id=1, source_target_pairs={{0,2},{2,0},{1,3},{3,1},{4,6},{6,4},{5,7},{7,5},{8,10},{10,8},{9,1... | collective-permute-start | bytes 3145736 | tf_op jit(solution)/shard_map/ppermute | solution.py:31
  226.4 38.7 %copy-start.40 = (bf16[512,1024]{1,0:T(8,128)(2,1)S(1)}, bf16[512,1024]{1,0:T(8,128)(2,1)}, u32[]{:S(2)}) copy-start(bf16[512,1024]{1,0:T(8,128)(2,1)} %all-gather.11.cloned.1.call-done) | copy-start | bytes 3145732
  227.4 40.6 %copy-start.43 = (bf16[512,1024]{1,0:T(8,128)(2,1)}, bf16[512,1024]{1,0:T(8,128)(2,1)S(1)}, u32[]{:S(2)}) copy-start(bf16[512,1024]{1,0:T(8,128)(2,1)S(1)} %add_convert_fusion) | copy-start | bytes 3145732
  227.4 40.6 %collective-permute-start.10 = (bf16[512,1024]{1,0:T(8,128)(2,1)S(1)}, bf16[512,1024]{1,0:T(8,128)(2,1)S(1)}, u32[]{:S(2)}, u32[]{:S(2)}) collective-permute-start(bf16[512,1024]{1,0:T(8,128)(2,1)S(1)} %add_convert_fusion), channel_id=1, source_target_pairs={{0,1},{1,0},{2,3},{3,2},{4,5},{5,4},{6,7},{7,6},{8,9},{9,8},{10,11... | collective-permute-start | bytes 3145736 | tf_op jit(solution)/shard_map/ppermute | solution.py:31
  291.2 48.9 %collective-permute-start.16 = (f32[512,1024]{1,0:T(8,128)}, f32[512,1024]{1,0:T(8,128)}, u32[]{:S(2)}, u32[]{:S(2)}) collective-permute-start(f32[512,1024]{1,0:T(8,128)} %slice.340), channel_id=1, source_target_pairs={{0,1},{1,0},{2,3},{3,2},{4,5},{5,4},{6,7},{7,6},{8,9},{9,8},{10,11... | collective-permute-start | bytes 6291464 | tf_op jit(solution)/shard_map/ppermute | solution.py:31
  299.6 40.5 %collective-permute-start.14 = (f32[512,1024]{1,0:T(8,128)}, f32[512,1024]{1,0:T(8,128)}, u32[]{:S(2)}, u32[]{:S(2)}) collective-permute-start(f32[512,1024]{1,0:T(8,128)} %slice.337), channel_id=1, source_target_pairs={{0,1},{1,0},{2,3},{3,2},{4,5},{5,4},{6,7},{7,6},{8,9},{9,8},{10,11... | collective-permute-start | bytes 6291464 | tf_op jit(solution)/shard_map/ppermute | solution.py:31
  309.8 26.3 %collective-permute-start.29 = (bf16[4,128,1024]{2,1,0:T(8,128)(2,1)}, bf16[4,128,1024]{2,1,0:T(8,128)(2,1)}, u32[]{:S(2)}, u32[]{:S(2)}) collective-permute-start(bf16[4,128,1024]{2,1,0:T(8,128)(2,1)} %get-tuple-element.88), channel_id=1, source_target_pairs={{0,2},{2,0},{1,3},{3,1},{4,6},{6,4},{5,7},{7,5},{8,10},{10,8},{9,1... | collective-permute-start | bytes 3145736 | tf_op jit(solution)/shard_map/ppermute | solution.py:31
  310.5 48.7 %collective-permute-start.28 = (bf16[4,128,1024]{2,1,0:T(8,128)(2,1)}, bf16[4,128,1024]{2,1,0:T(8,128)(2,1)}, u32[]{:S(2)}, u32[]{:S(2)}) collective-permute-start(bf16[4,128,1024]{2,1,0:T(8,128)(2,1)} %get-tuple-element.87), channel_id=1, source_target_pairs={{0,2},{2,0},{1,3},{3,1},{4,6},{6,4},{5,7},{7,5},{8,10},{10,8},{9,1... | collective-permute-start | bytes 3145736 | tf_op jit(solution)/shard_map/ppermute | solution.py:31
  338.6 24.7 %collective-permute-start.30 = (bf16[4,128,1024]{2,1,0:T(8,128)(2,1)}, bf16[4,128,1024]{2,1,0:T(8,128)(2,1)}, u32[]{:S(2)}, u32[]{:S(2)}) collective-permute-start(bf16[4,128,1024]{2,1,0:T(8,128)(2,1)} %bitcast_add_fusion.2), channel_id=1, source_target_pairs={{0,4},{4,0},{1,5},{5,1},{2,6},{6,2},{3,7},{7,3},{8,12},{12,8},{9,1... | collective-permute-start | bytes 3145736 | tf_op jit(solution)/shard_map/ppermute | solution.py:31
  357.0 9.4 %collective-permute-start.19 = (bf16[512,256]{1,0:T(8,128)(2,1)S(1)}, bf16[512,256]{1,0:T(8,128)(2,1)}, u32[]{:S(2)}, u32[]{:S(2)}) collective-permute-start(bf16[512,256]{1,0:T(8,128)(2,1)S(1)} %bitcast.295), channel_id=1, source_target_pairs={{0,3},{1,2},{2,1},{3,0},{4,7},{5,6},{6,5},{7,4},{8,11},{9,10},{10,... | collective-permute-start | bytes 786440 | tf_op jit(solution)/shard_map/ppermute | solution.py:365
  357.2 12.8 %collective-permute-start.18 = (bf16[512,256]{1,0:T(8,128)(2,1)S(1)}, bf16[512,256]{1,0:T(8,128)(2,1)}, u32[]{:S(2)}, u32[]{:S(2)}) collective-permute-start(bf16[512,256]{1,0:T(8,128)(2,1)S(1)} %bitcast.296), channel_id=1, source_target_pairs={{0,2},{2,0},{1,3},{3,1},{4,6},{6,4},{5,7},{7,5},{8,10},{10,8},{9,1... | collective-permute-start | bytes 786440 | tf_op jit(solution)/shard_map/ppermute | solution.py:31
  358.0 12.0 %collective-permute-start.17 = (bf16[512,256]{1,0:T(8,128)(2,1)S(1)}, bf16[512,256]{1,0:T(8,128)(2,1)}, u32[]{:S(2)}, u32[]{:S(2)}) collective-permute-start(bf16[512,256]{1,0:T(8,128)(2,1)S(1)} %bitcast.297), channel_id=1, source_target_pairs={{0,1},{1,0},{2,3},{3,2},{4,5},{5,4},{6,7},{7,6},{8,9},{9,8},{10,11... | collective-permute-start | bytes 786440 | tf_op jit(solution)/shard_map/ppermute | solution.py:31
  366.4 244.0 %reduce-scatter.4.cloned.1.call-start = ((), (), s32[]{:S(2)}) async-start(), calls=%async_computation.6 | async-start | bytes 1146880 | tf_op jit(solution)/shard_map/reduce_scatter | solution.py:450
  446.1 18.2 %collective-permute-start.20 = (bf16[2,512,1024]{2,1,0:T(8,128)(2,1)}, bf16[2,512,1024]{2,1,0:T(8,128)(2,1)}, u32[]{:S(2)}, u32[]{:S(2)}) collective-permute-start(bf16[2,512,1024]{2,1,0:T(8,128)(2,1)} %slice.289), channel_id=1, source_target_pairs={{0,1},{1,0},{2,3},{3,2},{4,5},{5,4},{6,7},{7,6},{8,9},{9,8},{10,11... | collective-permute-start | bytes 6291464 | tf_op jit(solution)/shard_map/ppermute | solution.py:31
  452.5 10.5 %collective-permute-start.23 = (bf16[1024,512]{1,0:T(8,128)(2,1)}, bf16[1024,512]{1,0:T(8,128)(2,1)}, u32[]{:S(2)}, u32[]{:S(2)}) collective-permute-start(bf16[1024,512]{1,0:T(8,128)(2,1)} %bitcast.284), channel_id=1, source_target_pairs={{0,1},{1,0},{2,3},{3,2},{4,5},{5,4},{6,7},{7,6},{8,9},{9,8},{10,11... | collective-permute-start | bytes 3145736 | tf_op jit(solution)/shard_map/ppermute | solution.py:31
  470.8 25.6 %collective-permute-start.21 = (bf16[512,1024]{1,0:T(8,128)(2,1)}, bf16[512,1024]{1,0:T(8,128)(2,1)}, u32[]{:S(2)}, u32[]{:S(2)}) collective-permute-start(bf16[512,1024]{1,0:T(8,128)(2,1)} %fusion.40), channel_id=1, source_target_pairs={{0,2},{2,0},{1,3},{3,1},{4,6},{6,4},{5,7},{7,5},{8,10},{10,8},{9,1... | collective-permute-start | bytes 3145736 | tf_op jit(solution)/shard_map/ppermute | solution.py:31
  476.5 31.9 %collective-permute-start.25 = (bf16[4,64,2560]{2,1,0:T(8,128)(2,1)}, bf16[4,64,2560]{2,1,0:T(8,128)(2,1)}, u32[]{:S(2)}, u32[]{:S(2)}) collective-permute-start(bf16[4,64,2560]{2,1,0:T(8,128)(2,1)} %get-tuple-element.82), channel_id=1, source_target_pairs={{0,4},{4,0},{1,5},{5,1},{2,6},{6,2},{3,7},{7,3},{8,12},{12,8},{9,1... | collective-permute-start | bytes 3932168 | tf_op jit(solution)/shard_map/ppermute | solution.py:31
  503.3 24.8 %collective-permute-start.22 = (bf16[4,128,896]{2,1,0:T(8,128)(2,1)}, bf16[4,128,896]{2,1,0:T(8,128)(2,1)}, u32[]{:S(2)}, u32[]{:S(2)}) collective-permute-start(bf16[4,128,896]{2,1,0:T(8,128)(2,1)} %fusion.56), channel_id=1, source_target_pairs={{0,4},{4,0},{1,5},{5,1},{2,6},{6,2},{3,7},{7,3},{8,12},{12,8},{9,1... | collective-permute-start | bytes 2752520 | tf_op jit(solution)/shard_map/ppermute | solution.py:31
  503.7 51.7 %collective-permute-start.24 = (bf16[4,64,2560]{2,1,0:T(8,128)(2,1)}, bf16[4,64,2560]{2,1,0:T(8,128)(2,1)}, u32[]{:S(2)}, u32[]{:S(2)}) collective-permute-start(bf16[4,64,2560]{2,1,0:T(8,128)(2,1)} %get-tuple-element.81), channel_id=1, source_target_pairs={{0,4},{4,0},{1,5},{5,1},{2,6},{6,2},{3,7},{7,3},{8,12},{12,8},{9,1... | collective-permute-start | bytes 3932168 | tf_op jit(solution)/shard_map/ppermute | solution.py:31
  511.4 44.0 %collective-permute-start.26 = (bf16[4,64,2560]{2,1,0:T(8,128)(2,1)}, bf16[4,64,2560]{2,1,0:T(8,128)(2,1)}, u32[]{:S(2)}, u32[]{:S(2)}) collective-permute-start(bf16[4,64,2560]{2,1,0:T(8,128)(2,1)} %bitcast_add_fusion), channel_id=1, source_target_pairs={{0,2},{2,0},{1,3},{3,1},{4,6},{6,4},{5,7},{7,5},{8,10},{10,8},{9,1... | collective-permute-start | bytes 3932168 | tf_op jit(solution)/shard_map/ppermute | solution.py:31
  530.5 28.4 %copy-start.2 = (f32[512,1024]{1,0:T(8,128)S(1)}, f32[512,1024]{1,0:T(8,128)}, u32[]{:S(2)}) copy-start(f32[512,1024]{1,0:T(8,128)} %copy-done) | copy-start | bytes 6291460
  530.5 83.3 %reduce-scatter.6.cloned.1.call-start = ((), (), s32[]{:S(2)}) async-start(), calls=%async_computation.7 | async-start | bytes 1638400 | tf_op jit(solution)/shard_map/reduce_scatter | solution.py:385
  610.4 9.0 %all-to-all-start.1 = ((bf16[4,32,896]{2,1,0:T(8,128)(2,1)}), bf16[4,32,896]{2,1,0:T(8,128)(2,1)S(1)}, u32[]{:S(2)}, u32[]{:S(2)}) async-start(bf16[4,32,896]{2,1,0:T(8,128)(2,1)} %bitcast.300), calls=%async_computation.2 | async-start | bytes 458752 | tf_op jit(solution)/shard_map/all_to_all | solution.py:451
  614.8 8.5 %collective-permute-start.27 = (bf16[32,2560]{1,0:T(8,128)(2,1)S(1)}, bf16[32,2560]{1,0:T(8,128)(2,1)S(1)}, u32[]{:S(2)}, u32[]{:S(2)}) collective-permute-start(bf16[32,2560]{1,0:T(8,128)(2,1)S(1)} %dynamic-slice_bitcast_fusion.4), channel_id=1, source_target_pairs={{0,1},{1,0},{2,3},{3,2},{4,5},{5,4},{6,7},{7,6},{8,9},{9,8},{10,11... | collective-permute-start | bytes 491528 | tf_op jit(solution)/shard_map/ppermute | solution.py:31
  (79 other events, 429.7 us)
Sparse Core Ops, SparseCore 0:
  9.6 30.6 all-gather.10
  42.4 32.1 all-gather.8
  77.3 52.8 all-gather.6
  366.5 25.5 reduce-scatter.7
  530.6 22.4 reduce-scatter.3
  559.0 28.9 reduce-scatter.5
